TPU v7x, 32 devices: a whole 2x2x4 slice. The times are simulated.
32 devices in a mesh: section: 2 (over y), dp: 8 (over z, x), tensor: 2 (over core).
Axes of the slice: x: 2, y: 2, z: 4, core: 2. Of those that a mesh axis runs over, the one named last changes fastest.
Arguments:
- layer_in: bfloat16 [2, 8, 256, 2048], P(None, 'dp', 'tensor', 'section'), may hold values from -6 to 6
- out_grad: bfloat16 [2, 8, 256, 2048], P(None, 'dp', 'tensor', 'section'), may hold values from -6 to 6
- doc_lengths: int32 [2, 8, 4], P(None, 'dp'), may hold values from 1 to 192, 256 in all within a row
- attn_gain: float32 [2, 2048], P('section'), may hold values from 0.1 to 1.9
- w_query: bfloat16 [2, 2048, 2048], P('section', 'dp', 'tensor'), may hold values from -0.125 to 0.125
- keyval_weight: bfloat16 [2, 2048, 2, 256], P('section', 'dp', None, 'tensor'), may hold values from -0.125 to 0.125
- w_out: bfloat16 [2, 2048, 2048], P('section', 'dp', 'tensor'), may hold values from -0.75 to 0.75
- mlp_gain: float32 [2, 2048], P('section'), may hold values from 0.1 to 1.9
- w_gate_up: bfloat16 [2, 2048, 2, 5632], P('section', 'dp', None, 'tensor'), may hold values from -0.125 to 0.125
- w_down: bfloat16 [2, 2048, 5632], P('section', 'dp', 'tensor'), may hold values from -0.078125 to 0.078125
Outputs:
- layer_out: bfloat16 [2, 8, 256, 2048], P(None, 'dp', 'tensor', 'section')
- in_grad: bfloat16 [2, 8, 256, 2048], P(None, 'dp', 'tensor', 'section')
- attn_gain_grad: float32 [2, 2048], P('section')
- w_query_grad: float32 [2, 2048, 2048], P('section', 'dp', 'tensor')
- w_keyval_grad: float32 [2, 2048, 2, 256], P('section', 'dp', None, 'tensor')
- w_out_grad: float32 [2, 2048, 2048], P('section', 'dp', 'tensor')
- mlp_gain_grad: float32 [2, 2048], P('section')
- w_gate_up_grad: float32 [2, 2048, 2, 5632], P('section', 'dp', None, 'tensor')
- w_down_grad: float32 [2, 2048, 5632], P('section', 'dp', 'tensor')
Inputs may be any that keep to these rules, and one draw needn't show every extreme that they name: `doc_lengths`: each sequence's 4 lengths sum to 256; its longest document has 192 tokens.
All inputs are finite; a program needn't handle non-finite values.
Results may differ from a plain program's by a relative error of at most 0.035.
Values may be sent and summed in bfloat16 or wider, within the bound.
A program may use at most 384 MiB of HBM per device.

v0:
```python
import jax
import jax.numpy as jnp
from jax import lax
from jax.sharding import PartitionSpec as P

HEAD_SIZE = 64
LEN = 256
MB = 2


NORM_EPSILON = 1e-05
ROPE_BASE = 10000.0
MASK_FILL = -1e30


def from_partner(block, axis, distance):
    count = lax.axis_size(axis)
    route = []
    for low in range(count):
        high = low | 1 << distance
        if high != low and high < count:
            route += [(low, high), (high, low)]
    return lax.ppermute(block, axis, route)


def passed_along(block, axis, distance):
    devices = range(lax.axis_size(axis))
    route = [(i - distance, i) for i in devices if i - distance in devices]
    return lax.ppermute(block, axis, route)


def rope_tables(token_length, head_width):
    middle_col = head_width // 2
    frequency = ROPE_BASE ** (-(jnp.arange(middle_col, dtype=jnp.float32) * 2.0) / head_width)
    angles = jnp.arange(token_length, dtype=jnp.float32)[:, None] * frequency[None, :]
    cosine_table = jnp.concatenate([jnp.cos(angles), jnp.cos(angles)], 1)
    sine_values = jnp.concatenate([jnp.sin(angles), jnp.sin(angles)], 1)
    return (cosine_table, sine_values)


def rotate_halves(values, cosine_table, sine_values):
    middle_col = values.shape[-1] // 2
    turned = jnp.concatenate([-values[..., middle_col:], values[..., :middle_col]], -1)
    return values * cosine_table[:, None, :] + turned * sine_values[:, None, :]


def unrotate(values, cosine_table, sine_values):
    middle_col = values.shape[-1] // 2
    sined = values * sine_values[:, None, :]
    turned = jnp.concatenate([sined[..., middle_col:], -sined[..., :middle_col]], -1)
    return values * cosine_table[:, None, :] + turned


def doc_mask(lengths, token_length):
    bounds = jnp.cumsum(lengths)
    places = jnp.arange(token_length, dtype=jnp.int32)
    owners = jnp.sum((places[:, None] >= bounds[None, :]).astype(jnp.int32), 1)
    return (owners[:, None] == owners[None, :]) & (places[None, :] <= places[:, None])


def norm_rows(values, gain_row):
    inverse = lax.rsqrt(jnp.mean(values * values, -1, keepdims=True) + NORM_EPSILON)
    return values * inverse * gain_row


def seq_gather(rows_here):
    return lax.all_gather(rows_here, "tensor", axis=0, tiled=True)


def seq_sum(partial_value):
    return lax.psum_scatter(
        partial_value.astype(jnp.bfloat16), "tensor", scatter_dimension=0, tiled=True
    ).astype(jnp.float32)


def project_out(activations, weight):
    return lax.dot_general(
        activations,
        lax.all_gather(weight, "dp", axis=0, tiled=True),
        (((1,), (1,)), ((), ())),
        preferred_element_type=jnp.float32,
    )


def back_out(gradient, weight):
    return jnp.dot(
        gradient,
        lax.all_gather(weight, "dp", axis=0, tiled=True),
        preferred_element_type=jnp.float32,
    )


def weight_term(left_rows, right_rows):
    return lax.psum_scatter(
        lax.dot_general(
            left_rows, right_rows, (((0,), (0,)), ((), ())), preferred_element_type=jnp.float32
        ).astype(jnp.bfloat16),
        "dp",
        scatter_dimension=0,
        tiled=True,
    ).astype(jnp.float32)


def layer_forward(entering, params, visible, cosine_table, sine_values):
    attn_gain, w_query, keyval_weight, w_out, mlp_gain, w_gate_up, w_down = params
    normed = norm_rows(entering, attn_gain).astype(jnp.bfloat16)
    gathered = seq_gather(normed)
    rows_all = gathered.shape[0]
    columns = gathered
    query_sum = jnp.dot(
        columns,
        lax.all_gather(w_query, "dp", axis=0, tiled=True),
        preferred_element_type=jnp.float32,
    )
    keyval_sum = jnp.einsum(
        "td,dkc->tkc",
        columns,
        lax.all_gather(keyval_weight, "dp", axis=0, tiled=True),
        preferred_element_type=jnp.float32,
    )
    heads_q = w_query.shape[1] // HEAD_SIZE
    heads_kv = keyval_weight.shape[2] // HEAD_SIZE
    query_groups = heads_q // heads_kv
    factor = HEAD_SIZE ** (-0.5)
    rotated_queries = (
        rotate_halves(query_sum.reshape(rows_all, heads_q, HEAD_SIZE), cosine_table, sine_values)
        .astype(jnp.bfloat16)
        .reshape(rows_all, heads_kv, query_groups, HEAD_SIZE)
    )
    rotated_keys = rotate_halves(
        keyval_sum[:, 0].reshape(rows_all, heads_kv, HEAD_SIZE), cosine_table, sine_values
    ).astype(jnp.bfloat16)
    value_lower_half = keyval_sum[:, 1].reshape(rows_all, heads_kv, HEAD_SIZE).astype(jnp.bfloat16)
    scores = (
        jnp.einsum(
            "lhgc,mhc->hglm", rotated_queries, rotated_keys, preferred_element_type=jnp.float32
        )
        * factor
    )
    masked = jnp.where(visible, scores, MASK_FILL)
    row_max = jnp.max(masked, -1, keepdims=True)
    exponent = jnp.exp(masked - row_max)
    totals = jnp.sum(exponent, -1, keepdims=True)
    softmax_rows = exponent / totals
    log_total = row_max + jnp.log(totals)
    attended = jnp.einsum(
        "hglm,mhc->lhgc",
        softmax_rows.astype(jnp.bfloat16),
        value_lower_half,
        preferred_element_type=jnp.float32,
    )
    att_low = attended.reshape(rows_all, heads_q * HEAD_SIZE).astype(jnp.bfloat16)
    middle = entering + seq_sum(project_out(att_low, w_out))
    normed_mlp = norm_rows(middle, mlp_gain).astype(jnp.bfloat16)
    gathered_mlp = seq_gather(normed_mlp)
    columns = gathered_mlp
    gate_up = jnp.einsum(
        "td,dkf->tkf",
        columns,
        lax.all_gather(w_gate_up, "dp", axis=0, tiled=True),
        preferred_element_type=jnp.float32,
    )
    hidden = (jax.nn.silu(gate_up[:, 0]) * gate_up[:, 1]).astype(jnp.bfloat16)
    leaving = middle + seq_sum(project_out(hidden, w_down))
    stored = (
        entering,
        middle,
        gathered,
        att_low,
        gathered_mlp,
        gate_up,
        hidden,
        rotated_queries,
        rotated_keys,
        value_lower_half,
        log_total,
        visible,
    )
    return (leaving, stored)


def layer_backward(incoming, params, stored, cosine_table, sine_values):
    attn_gain, w_query, keyval_weight, w_out, mlp_gain, w_gate_up, w_down = params
    (
        entering,
        middle,
        gathered,
        att_low,
        gathered_mlp,
        gate_up,
        hidden,
        rotated_queries,
        rotated_keys,
        value_lower_half,
        log_total,
        visible,
    ) = stored
    rows_all = gathered.shape[0]
    heads_kv = rotated_keys.shape[1]
    query_groups = rotated_queries.shape[2]
    heads_q = heads_kv * query_groups
    factor = HEAD_SIZE ** (-0.5)
    grad_mlp = seq_gather(incoming.astype(jnp.bfloat16))
    grad_hidden = back_out(grad_mlp, w_down).astype(jnp.bfloat16)
    gate_part = gate_up[:, 0]
    up_part = gate_up[:, 1]
    sigmoid_gate = jax.nn.sigmoid(gate_part)
    grad_gate = grad_hidden * up_part * sigmoid_gate * (1.0 + gate_part * (1.0 - sigmoid_gate))
    grad_up = grad_hidden * (gate_part * sigmoid_gate)
    grad_gate_up = jnp.stack([grad_gate, grad_up], 1).astype(jnp.bfloat16)
    contribution = jnp.einsum(
        "tkf,dkf->td",
        grad_gate_up,
        lax.all_gather(w_gate_up, "dp", axis=0, tiled=True),
        preferred_element_type=jnp.float32,
    )
    grad_normed_mlp = seq_sum(contribution)
    unused_mlp, norm_back_mlp = jax.vjp(norm_rows, middle, mlp_gain)
    grad_middle_norm, grad_mlp_gain = norm_back_mlp(grad_normed_mlp)
    grad_middle = incoming + grad_middle_norm
    grad_branch = seq_gather(grad_middle.astype(jnp.bfloat16))
    grad_att = (
        back_out(grad_branch, w_out)
        .astype(jnp.bfloat16)
        .reshape(rows_all, heads_kv, query_groups, HEAD_SIZE)
    )
    scores = (
        jnp.einsum(
            "lhgc,mhc->hglm", rotated_queries, rotated_keys, preferred_element_type=jnp.float32
        )
        * factor
    )
    masked = jnp.where(visible, scores, MASK_FILL)
    softmax_rows = jnp.exp(masked - log_total)
    grad_value = jnp.einsum(
        "hglm,lhgc->mhc",
        softmax_rows.astype(jnp.bfloat16),
        grad_att,
        preferred_element_type=jnp.float32,
    )
    grad_soft = jnp.einsum(
        "lhgc,mhc->hglm", grad_att, value_lower_half, preferred_element_type=jnp.float32
    )
    row_inner = jnp.sum(softmax_rows * grad_soft, -1, keepdims=True)
    grad_scores = (softmax_rows * (grad_soft - row_inner) * factor).astype(jnp.bfloat16)
    grad_query_rot = jnp.einsum(
        "hglm,mhc->lhgc", grad_scores, rotated_keys, preferred_element_type=jnp.float32
    ).reshape(rows_all, heads_q, HEAD_SIZE)
    grad_key_rot = jnp.einsum(
        "hglm,lhgc->mhc", grad_scores, rotated_queries, preferred_element_type=jnp.float32
    )
    grad_query = (
        unrotate(grad_query_rot, cosine_table, sine_values)
        .reshape(rows_all, heads_q * HEAD_SIZE)
        .astype(jnp.bfloat16)
    )
    grad_key = unrotate(grad_key_rot, cosine_table, sine_values).reshape(
        rows_all, heads_kv * HEAD_SIZE
    )
    grad_keyval = jnp.stack(
        [grad_key, grad_value.reshape(rows_all, heads_kv * HEAD_SIZE)], 1
    ).astype(jnp.bfloat16)
    contribution = lax.dot_general(
        grad_query,
        lax.all_gather(w_query, "dp", axis=0, tiled=True),
        (((1,), (1,)), ((), ())),
        preferred_element_type=jnp.float32,
    )
    contribution = contribution + jnp.einsum(
        "tkc,dkc->td",
        grad_keyval,
        lax.all_gather(keyval_weight, "dp", axis=0, tiled=True),
        preferred_element_type=jnp.float32,
    )
    grad_normed = seq_sum(contribution)
    unused_attn, norm_back_attn = jax.vjp(norm_rows, entering, attn_gain)
    grad_entering_norm, grad_attn_gain = norm_back_attn(grad_normed)
    grad_entering = grad_middle + grad_entering_norm
    grad_qkv = jnp.concatenate([grad_query, grad_keyval.reshape(rows_all, -1)], 1)
    pair_list = (
        gathered,
        grad_qkv,
        grad_branch,
        att_low,
        gathered_mlp,
        grad_gate_up.reshape(rows_all, -1),
        grad_mlp,
        hidden,
    )
    return (grad_entering, (grad_attn_gain, grad_mlp_gain), pair_list)


def weight_grads(pair_list, params):
    gathered, grad_qkv, grad_branch, att_low, gathered_mlp, grad_gate_up, grad_mlp, hidden = (
        pair_list
    )
    query_cols = params[1].shape[1]
    term_qkv = weight_term(gathered, grad_qkv)
    grad_w_query = term_qkv[:, :query_cols]
    grad_w_keyval = term_qkv[:, query_cols:].reshape(params[2].shape)
    grad_w_out = weight_term(grad_branch, att_low)
    grad_w_gate_up = weight_term(gathered_mlp, grad_gate_up).reshape(params[5].shape)
    grad_w_down = weight_term(grad_mlp, hidden)
    return (grad_w_query, grad_w_keyval, grad_w_out, grad_w_gate_up, grad_w_down)


def shards(
    layer_in,
    out_grad,
    doc_lengths,
    attn_gain,
    w_query,
    keyval_weight,
    w_out,
    mlp_gain,
    w_gate_up,
    w_down,
):
    section_index = lax.axis_index("section")
    first_section = section_index == 0
    outbound = jnp.where(first_section, out_grad, layer_in)
    returned = from_partner(outbound, "section", 0)
    low_half = jnp.where(first_section, layer_in, returned)
    high_half = jnp.where(first_section, returned, out_grad)
    entries = jnp.concatenate([low_half, high_half], 3)
    params = (
        attn_gain[0],
        w_query[0],
        keyval_weight[0],
        w_out[0],
        mlp_gain[0],
        w_gate_up[0],
        w_down[0],
    )
    cosine_table, sine_values = rope_tables(LEN, HEAD_SIZE)
    masks = [doc_mask(doc_lengths[batch_index, 0], LEN) for batch_index in range(MB)]
    received = jnp.zeros(entries.shape[2:], jnp.bfloat16)
    stored_ticks = []
    sent_ticks = []
    for moment in range(MB + 1):
        visible = jnp.where(first_section, masks[min(moment, MB - 1)], masks[max(moment - 1, 0)])
        entering = jnp.where(first_section, entries[min(moment, MB - 1), 0], received).astype(
            jnp.float32
        )
        leaving, stored = layer_forward(entering, params, visible, cosine_table, sine_values)
        stored_ticks.append(stored)
        handed = leaving.astype(jnp.bfloat16)
        sent_ticks.append(handed)
        if moment < MB:
            received = passed_along(handed, "section", 1)
    received = jnp.zeros(entries.shape[2:], jnp.bfloat16)
    width_model = entries.shape[3]
    gain_totals = (jnp.zeros((width_model,), jnp.float32), jnp.zeros((width_model,), jnp.float32))
    back_ticks = []
    weight_totals = None
    for moment in range(MB + 1):
        stored = jax.tree.map(
            lambda for_second, for_first: jnp.where(first_section, for_first, for_second),
            stored_ticks[min(moment + 1, MB)],
            stored_ticks[max(moment - 1, 0)],
        )
        incoming = jnp.where(first_section, received, entries[min(moment, MB - 1), 0]).astype(
            jnp.float32
        )
        grad_entering, gain_grads, pair_list = layer_backward(
            incoming, params, stored, cosine_table, sine_values
        )
        useful = jnp.where(first_section, moment >= 1, moment < MB)
        useful_full = useful.astype(jnp.float32)
        gain_totals = (
            gain_totals[0] + useful_full * gain_grads[0],
            gain_totals[1] + useful_full * gain_grads[1],
        )
        handed = grad_entering.astype(jnp.bfloat16)
        back_ticks.append(handed)
        if moment < MB:
            received = passed_along(handed, "section", -1)
        useful_low = useful.astype(jnp.bfloat16)
        masked_pairs = tuple(
            (
                member * useful_low if position in (1, 2, 5, 6) else member
                for position, member in enumerate(pair_list)
            )
        )
        grads_now = weight_grads(masked_pairs, params)
        if weight_totals is None:
            weight_totals = grads_now
        else:
            weight_totals = tuple((older + newer for older, newer in zip(weight_totals, grads_now)))
    finished = jnp.stack(
        [
            jnp.where(first_section, back_ticks[batch_index + 1], sent_ticks[batch_index + 1])
            for batch_index in range(MB)
        ]
    )[:, None]
    middle_col = finished.shape[3] // 2
    outbound = jnp.where(first_section, finished[..., middle_col:], finished[..., :middle_col])
    returned = from_partner(outbound, "section", 0)
    layer_out = jnp.where(first_section, returned, finished[..., middle_col:])
    in_grad = jnp.where(first_section, finished[..., :middle_col], returned)
    gain_summed = lax.psum((gain_totals[0], gain_totals[1]), ("dp", "tensor"))
    grad_w_query, grad_w_keyval, grad_w_out, grad_w_gate_up, grad_w_down = weight_totals
    return (
        layer_out,
        in_grad,
        gain_summed[0][None],
        grad_w_query[None],
        grad_w_keyval[None],
        grad_w_out[None],
        gain_summed[1][None],
        grad_w_gate_up[None],
        grad_w_down[None],
    )


def solution(mesh):
    return jax.shard_map(
        shards,
        mesh=mesh,
        in_specs=(
            P(None, "dp", "tensor", "section"),
            P(None, "dp", "tensor", "section"),
            P(None, "dp", None),
            P("section", None),
            P("section", "dp", "tensor"),
            P("section", "dp", None, "tensor"),
            P("section", "dp", "tensor"),
            P("section", None),
            P("section", "dp", None, "tensor"),
            P("section", "dp", "tensor"),
        ),
        out_specs=(
            P(None, "dp", "tensor", "section"),
            P(None, "dp", "tensor", "section"),
            P("section", None),
            P("section", "dp", "tensor"),
            P("section", "dp", None, "tensor"),
            P("section", "dp", "tensor"),
            P("section", None),
            P("section", "dp", None, "tensor"),
            P("section", "dp", "tensor"),
        ),
        check_vma=False,
    )
```

profile of v0, /device:TPU:0, one launch (start us, length us, event | category | flops | bytes accessed | tf_op | source)
XLA Modules:
  0.0 3714.0 jit_solution(8164840932734129476)
XLA Ops:
  37.7 43.4 %all-gather.50.cloned.1.call-done = bf16[1,2048,2,128]{1,3,2,0:T(8,128)(2,1)} async-done(((bf16[1,256,2,128]{1,3,2,0:T(8,128)(2,1)}), bf16[1,2048,2,128]{1,3,2,0:T(8,128)(2,1)}) %all-gather.50.cloned.1.call-update) | async-done | bytes 1048592 | tf_op jit(solution)/shard_map/all_gather | solution.py:118
  83.7 71.7 %all-gather.52.cloned.1.call-done = bf16[1,2048,1024]{2,1,0:T(8,128)(2,1)} async-done(((bf16[1,256,1024]{2,1,0:T(8,128)(2,1)}), bf16[1,2048,1024]{2,1,0:T(8,128)(2,1)}) %all-gather.52.cloned.1.call-update) | async-done | bytes 4194320 | tf_op jit(solution)/shard_map/all_gather | solution.py:112
  163.0 66.1 %all-gather.54.cloned.1.call-done = bf16[1,2048,1024]{2,1,0:T(8,128)(2,1)} async-done(((bf16[1,256,1024]{2,1,0:T(8,128)(2,1)}), bf16[1,2048,1024]{2,1,0:T(8,128)(2,1)}) %all-gather.54.cloned.1.call-update) | async-done | bytes 4194320 | tf_op jit(solution)/shard_map/all_gather | solution.py:79
  254.4 444.5 %all-gather.56.cloned.1.call-done = bf16[1,2048,2,2816]{3,1,2,0:T(8,128)(2,1)} async-done(((bf16[1,256,2,2816]{3,1,2,0:T(8,128)(2,1)}), bf16[1,2048,2,2816]{3,1,2,0:T(8,128)(2,1)}) %all-gather.56.cloned.1.call-update) | async-done | bytes 23068688 | tf_op jit(solution)/shard_map/all_gather | solution.py:160
  713.4 151.6 %all-gather.48.cloned.1.call-done = bf16[1,2048,2816]{2,1,0:T(8,128)(2,1)} async-done(((bf16[1,256,2816]{2,1,0:T(8,128)(2,1)}), bf16[1,2048,2816]{2,1,0:T(8,128)(2,1)}) %all-gather.48.cloned.1.call-update) | async-done | bytes 11534352 | tf_op jit(solution)/shard_map/all_gather | solution.py:88
  949.7 15.3 broadcast_select_fusion.2
  1111.0 14.8 collective-permute-done.2
  1127.1 21.3 broadcast_select_fusion
  1252.1 14.6 collective-permute-done.4
  1437.6 12.7 convolution_convert_fusion.2
  1459.5 13.3 convolution_convert_fusion.1
  1477.7 12.9 convolution_convert_fusion
  1499.5 64.6 %all-reduce = (f32[1,2048]{1,0:T(1,128)}, f32[1,2048]{1,0:T(1,128)}) all-reduce(f32[1,2048]{1,0:T(1,128)S(1)} %bitcast.845, f32[1,2048]{1,0:T(1,128)S(1)} %bitcast.844), channel_id=1, replica_groups=mesh['section'=2,'dp'=8,'tensor'=2] {'dp','tensor'}, use_global_device_ids=true, to_apply=%region_46.47 | all-reduce | flops 4096 | bytes 32768 | tf_op jit(solution)/shard_map/psum | solution.py:401
  1565.1 26.8 reduce-scatter.51.cloned.1.call-done
  1594.2 89.2 %reduce-scatter.55.cloned.1.call-done = bf16[256,1024]{1,0:T(8,128)(2,1)} async-done(((bf16[2048,1024]{1,0:T(8,128)(2,1)}), bf16[256,1024]{1,0:T(8,128)(2,1)}) %reduce-scatter.55.cloned.1.call-update) | async-done | bytes 524304 | tf_op jit(solution)/shard_map/reduce_scatter | solution.py:94
  1683.4 91.6 %reduce-scatter.57.cloned.1.call-done = bf16[256,1024]{1,0:T(8,128)(2,1)} async-done(((bf16[2048,1024]{1,0:T(8,128)(2,1)}), bf16[256,1024]{1,0:T(8,128)(2,1)}) %reduce-scatter.57.cloned.1.call-update) | async-done | bytes 524304 | tf_op jit(solution)/shard_map/reduce_scatter | solution.py:94
  1775.1 91.5 %reduce-scatter.59.cloned.1.call-done = bf16[256,1024]{1,0:T(8,128)(2,1)} async-done(((bf16[2048,1024]{1,0:T(8,128)(2,1)}), bf16[256,1024]{1,0:T(8,128)(2,1)}) %reduce-scatter.59.cloned.1.call-update) | async-done | bytes 524304 | tf_op jit(solution)/shard_map/reduce_scatter | solution.py:94
  1869.2 104.3 %reduce-scatter.53.cloned.1.call-done = bf16[256,1280]{1,0:T(8,128)(2,1)} async-done(((bf16[2048,1280]{1,0:T(8,128)(2,1)}), bf16[256,1280]{1,0:T(8,128)(2,1)}) %reduce-scatter.53.cloned.1.call-update) | async-done | bytes 655376 | tf_op jit(solution)/shard_map/reduce_scatter | solution.py:94
  1980.4 189.5 %reduce-scatter.67.cloned.1.call-done = bf16[256,2816]{1,0:T(8,128)(2,1)} async-done(((bf16[2048,2816]{1,0:T(8,128)(2,1)}), bf16[256,2816]{1,0:T(8,128)(2,1)}) %reduce-scatter.67.cloned.1.call-update) | async-done | bytes 1441808 | tf_op jit(solution)/shard_map/reduce_scatter | solution.py:94
  2169.8 195.7 %reduce-scatter.69.cloned.1.call-done = bf16[256,2816]{1,0:T(8,128)(2,1)} async-done(((bf16[2048,2816]{1,0:T(8,128)(2,1)}), bf16[256,2816]{1,0:T(8,128)(2,1)}) %reduce-scatter.69.cloned.1.call-update) | async-done | bytes 1441808 | tf_op jit(solution)/shard_map/reduce_scatter | solution.py:94
  2365.5 195.8 %reduce-scatter.71.cloned.1.call-done = bf16[256,2816]{1,0:T(8,128)(2,1)} async-done(((bf16[2048,2816]{1,0:T(8,128)(2,1)}), bf16[256,2816]{1,0:T(8,128)(2,1)}) %reduce-scatter.71.cloned.1.call-update) | async-done | bytes 1441808 | tf_op jit(solution)/shard_map/reduce_scatter | solution.py:94
  2565.6 372.2 %reduce-scatter.61.cloned.1.call-done = bf16[256,5632]{1,0:T(8,128)(2,1)} async-done(((bf16[2048,5632]{1,0:T(8,128)(2,1)}), bf16[256,5632]{1,0:T(8,128)(2,1)}) %reduce-scatter.61.cloned.1.call-update) | async-done | bytes 2883600 | tf_op jit(solution)/shard_map/reduce_scatter | solution.py:94
  2937.8 377.0 %reduce-scatter.63.cloned.1.call-done = bf16[256,5632]{1,0:T(8,128)(2,1)} async-done(((bf16[2048,5632]{1,0:T(8,128)(2,1)}), bf16[256,5632]{1,0:T(8,128)(2,1)}) %reduce-scatter.63.cloned.1.call-update) | async-done | bytes 2883600 | tf_op jit(solution)/shard_map/reduce_scatter | solution.py:94
  3314.8 377.0 %reduce-scatter.65.cloned.1.call-done = bf16[256,5632]{1,0:T(8,128)(2,1)} async-done(((bf16[2048,5632]{1,0:T(8,128)(2,1)}), bf16[256,5632]{1,0:T(8,128)(2,1)}) %reduce-scatter.65.cloned.1.call-update) | async-done | bytes 2883600 | tf_op jit(solution)/shard_map/reduce_scatter | solution.py:94
  (563 shorter events, 639.6 us)
Async XLA Ops:
  27.9 127.6 %all-gather.52.cloned.1.call-start = ((), (), s32[]{:S(2)}) async-start(), calls=%async_computation.62 | async-start | bytes 4718592 | tf_op jit(solution)/shard_map/all_gather | solution.py:112
  28.6 200.6 %all-gather.54.cloned.1.call-start = ((), (), s32[]{:S(2)}) async-start(), calls=%async_computation.63 | async-start | bytes 4718592 | tf_op jit(solution)/shard_map/all_gather | solution.py:79
  29.2 211.4 %reduce-scatter.25.cloned.1.call-start = ((), (), s32[]{:S(2)}) async-start(), calls=%async_computation.25 | async-start | bytes 1572864 | tf_op jit(solution)/shard_map/reduce_scatter | solution.py:71
  244.0 454.9 %all-gather.56.cloned.1.call-start = ((), (), s32[]{:S(2)}) async-start(), calls=%async_computation.64 | async-start | bytes 25952256 | tf_op jit(solution)/shard_map/all_gather | solution.py:160
  247.8 617.2 %all-gather.48.cloned.1.call-start = ((), (), s32[]{:S(2)}) async-start(), calls=%async_computation.60 | async-start | bytes 12976128 | tf_op jit(solution)/shard_map/all_gather | solution.py:88
  248.5 631.8 %reduce-scatter.27.cloned.1.call-start = ((), (), s32[]{:S(2)}) async-start(), calls=%async_computation.27 | async-start | bytes 1572864 | tf_op jit(solution)/shard_map/reduce_scatter | solution.py:71
  940.3 66.8 %reduce-scatter.31.cloned.1.call-start = ((), (), s32[]{:S(2)}) async-start(), calls=%async_computation.31 | async-start | bytes 1572864 | tf_op jit(solution)/shard_map/reduce_scatter | solution.py:71
  1030.4 62.0 %reduce-scatter.33.cloned.1.call-start = ((), (), s32[]{:S(2)}) async-start(), calls=%async_computation.33 | async-start | bytes 1572864 | tf_op jit(solution)/shard_map/reduce_scatter | solution.py:71
  1187.5 57.7 %reduce-scatter.41.cloned.1.call-start = ((), (), s32[]{:S(2)}) async-start(), calls=%async_computation.41 | async-start | bytes 1572864 | tf_op jit(solution)/shard_map/reduce_scatter | solution.py:71
  1315.0 176.2 %reduce-scatter.45.cloned.1.call-start = ((), (), s32[]{:S(2)}) async-start(), calls=%async_computation.45 | async-start | bytes 1572864 | tf_op jit(solution)/shard_map/reduce_scatter | solution.py:71
  1354.4 139.0 %reduce-scatter.47.cloned.1.call-start = ((), (), s32[]{:S(2)}) async-start(), calls=%async_computation.46 | async-start | bytes 1572864 | tf_op jit(solution)/shard_map/reduce_scatter | solution.py:71
  1368.1 130.1 %reduce-scatter.49.cloned.1.call-start = ((), (), s32[]{:S(2)}) async-start(), calls=%async_computation.47 | async-start | bytes 5898240 | tf_op jit(solution)/shard_map/reduce_scatter | solution.py:94
  1372.5 219.4 %reduce-scatter.51.cloned.1.call-start = ((), (), s32[]{:S(2)}) async-start(), calls=%async_computation.48 | async-start | bytes 5898240 | tf_op jit(solution)/shard_map/reduce_scatter | solution.py:94
  1380.2 303.3 %reduce-scatter.55.cloned.1.call-start = ((), (), s32[]{:S(2)}) async-start(), calls=%async_computation.50 | async-start | bytes 4718592 | tf_op jit(solution)/shard_map/reduce_scatter | solution.py:94
  1385.7 389.4 %reduce-scatter.57.cloned.1.call-start = ((), (), s32[]{:S(2)}) async-start(), calls=%async_computation.51 | async-start | bytes 4718592 | tf_op jit(solution)/shard_map/reduce_scatter | solution.py:94
  1391.2 475.4 %reduce-scatter.59.cloned.1.call-start = ((), (), s32[]{:S(2)}) async-start(), calls=%async_computation.52 | async-start | bytes 4718592 | tf_op jit(solution)/shard_map/reduce_scatter | solution.py:94
  1396.8 576.7 %reduce-scatter.53.cloned.1.call-start = ((), (), s32[]{:S(2)}) async-start(), calls=%async_computation.49 | async-start | bytes 5898240 | tf_op jit(solution)/shard_map/reduce_scatter | solution.py:94
  1401.8 768.0 %reduce-scatter.67.cloned.1.call-start = ((), (), s32[]{:S(2)}) async-start(), calls=%async_computation.56 | async-start | bytes 12976128 | tf_op jit(solution)/shard_map/reduce_scatter | solution.py:94
  1411.3 954.3 %reduce-scatter.69.cloned.1.call-start = ((), (), s32[]{:S(2)}) async-start(), calls=%async_computation.57 | async-start | bytes 12976128 | tf_op jit(solution)/shard_map/reduce_scatter | solution.py:94
  1420.3 1141.1 %reduce-scatter.71.cloned.1.call-start = ((), (), s32[]{:S(2)}) async-start(), calls=%async_computation.58 | async-start | bytes 12976128 | tf_op jit(solution)/shard_map/reduce_scatter | solution.py:94
  1429.2 1508.6 %reduce-scatter.61.cloned.1.call-start = ((), (), s32[]{:S(2)}) async-start(), calls=%async_computation.53 | async-start | bytes 25952256 | tf_op jit(solution)/shard_map/reduce_scatter | solution.py:94
  1450.3 1864.5 %reduce-scatter.63.cloned.1.call-start = ((), (), s32[]{:S(2)}) async-start(), calls=%async_computation.54 | async-start | bytes 25952256 | tf_op jit(solution)/shard_map/reduce_scatter | solution.py:94
  1472.8 2219.0 %reduce-scatter.65.cloned.1.call-start = ((), (), s32[]{:S(2)}) async-start(), calls=%async_computation.55 | async-start | bytes 25952256 | tf_op jit(solution)/shard_map/reduce_scatter | solution.py:94
  1496.0 68.1 %collective-permute-start.5 = (bf16[2,1,128,1024]{3,2,0,1:T(8,128)(2,1)S(1)}, bf16[2,1,128,1024]{3,2,0,1:T(8,128)(2,1)S(1)}, u32[]{:S(2)}, u32[]{:S(2)}) collective-permute-start(bf16[2,1,128,1024]{3,2,0,1:T(8,128)(2,1)S(1)} %broadcast_select_fusion.12), channel_id=1, source_target_pairs={{0,16},{16,0},{1,17},{17,1},{2,18},{18,2},{3,19},{19,3},{4,20},{20... | collective-permute-start | bytes 1572872 | tf_op jit(solution)/shard_map/ppermute | solution.py:23
  (148 other events, 2295.0 us)
Sparse Core Ops, SparseCore 0:
  27.1 10.4 all-gather.23
  40.3 40.6 all-gather.49
  83.1 72.2 all-gather.51
  157.4 71.6 all-gather.53
  244.2 10.2 all-gather.25
  256.6 442.2 all-gather.55
  701.3 163.6 all-gather.47
  900.0 10.9 all-gather.27
  951.9 10.1 all-gather.45
  1030.5 11.0 all-gather.35
  1080.1 10.6 reduce-scatter.32
  1315.2 10.1 all-gather.43
  1381.4 103.7 reduce-scatter.48
  1488.7 103.1 reduce-scatter.50
  1595.6 87.7 reduce-scatter.54
  1687.4 87.6 reduce-scatter.56
  1778.7 87.8 reduce-scatter.58
  1871.2 102.3 reduce-scatter.52
  1977.4 192.4 reduce-scatter.66
  2173.7 191.7 reduce-scatter.68
  2369.5 191.7 reduce-scatter.70
  2565.6 372.1 reduce-scatter.60
  2942.2 372.6 reduce-scatter.62
  3319.2 372.6 reduce-scatter.64
  (17 shorter events, 156.0 us)
where the time goes:
time: 3720 us; the launch traced here: 3710 us
  waiting for transfers between devices  3070 us (83%)
  matrix products  369 us (10%)
  other arithmetic  111 us (3%)
  blocking collectives  64.6 us (2%)
  local copies, waits for them, and re-layouts  63.3 us (2%)
    reduce_scatter x12, waiting for transfers between devices, weight_term(): lax.psum_scatter(lax.dot_general(left_rows, right_rows, (((0,), (0,)), ((...  2110 us
    all_gather x1, waiting for transfers between devices, layer_forward(): lax.all_gather(w_gate_up, 'dp', axis=0, tiled=True)  444 us
    all_gather x1, waiting for transfers between devices, back_out(): lax.all_gather(weight, 'dp', axis=0, tiled=True)  152 us
    dot_general x12, matrix products, weight_term(): lax.dot_general(left_rows, right_rows, (((0,), (0,)), ((), ())), preferre...  88.8 us
  transfers between devices with their start and end apart: 47, of which 36 were waited for; matrix products, arithmetic and copies ran while one was open for 8% of the time, Pallas kernels for 0%

commit v1 on v0

v1 whole, which is shorter than its diff:
```python
import functools

import jax
import jax.numpy as jnp
from jax import lax
from jax.experimental import pallas as pl
from jax.experimental.pallas import tpu as pltpu
from jax.sharding import PartitionSpec as P

HEAD_SIZE = 64
NORM_EPSILON = 1e-05
ROPE_BASE = 10000.0
MASK_FILL = -1e30
FACTOR = HEAD_SIZE ** (-0.5)
BF16 = jnp.bfloat16
F32 = jnp.float32

TENSOR = ("tensor", 0)
SECTION = ("section", 0)
SHARED = ("dp", 1)


def swap(block, place):
    axis, bit = place
    count = lax.axis_size(axis)
    return lax.ppermute(block, axis, [(i, i ^ (1 << bit)) for i in range(count)])


def side(place):
    axis, bit = place
    return (lax.axis_index(axis) >> bit) & 1


def pair(own, other, place, axis=0):
    first = side(place) == 0
    low = jnp.where(first, own, other)
    high = jnp.where(first, other, own)
    return jnp.stack([low, high], axis)


def pick(halves, which, axis):
    return lax.dynamic_index_in_dim(halves, which, axis, keepdims=False)


def dp_bits():
    count = lax.axis_size("dp")
    return [("dp", bit) for bit in reversed(range(count.bit_length() - 1))]


def rope_tables(token_length):
    middle = HEAD_SIZE // 2
    frequency = ROPE_BASE ** (-(jnp.arange(middle, dtype=F32) * 2.0) / HEAD_SIZE)
    angles = frequency[:, None] * jnp.arange(token_length, dtype=F32)[None, :]
    return (
        jnp.concatenate([jnp.cos(angles), jnp.cos(angles)], 0),
        jnp.concatenate([jnp.sin(angles), jnp.sin(angles)], 0),
    )


def owners_of(lengths, token_length):
    bounds = jnp.cumsum(lengths, -1)
    places = jnp.arange(token_length, dtype=jnp.int32)
    return jnp.sum((places[None, :, None] >= bounds[:, None, :]).astype(jnp.int32), -1)


def visible_block(owner_col, owner_row):
    length = owner_col.shape[0]
    key_place = lax.broadcasted_iota(jnp.int32, (length, length), 0)
    query_place = lax.broadcasted_iota(jnp.int32, (length, length), 1)
    return (owner_col == owner_row) & (key_place <= query_place)


def rope(u, cosine, sine):
    half = HEAD_SIZE // 2
    return u * cosine + jnp.concatenate([-u[half:], u[:half]], 0) * sine


def rope_back(u, cosine, sine):
    half = HEAD_SIZE // 2
    w = u * sine
    return u * cosine + jnp.concatenate([w[half:], -w[:half]], 0)


def attention_kernel(heads, qkv, cosine, sine, owner_col, owner_row, rotated, attended, log_total):
    cos, sin = cosine[...], sine[...]
    width = heads * HEAD_SIZE
    visible = visible_block(owner_col[0], owner_row[0])
    keys = rope(qkv[width : width + HEAD_SIZE, :], cos, sin).astype(BF16)
    values = qkv[width + HEAD_SIZE :, :].astype(BF16)
    rotated[width : width + HEAD_SIZE, :] = keys
    rotated[width + HEAD_SIZE :, :] = values
    for h in range(heads):
        at = slice(h * HEAD_SIZE, (h + 1) * HEAD_SIZE)
        queries = rope(qkv[at, :], cos, sin).astype(BF16)
        rotated[at, :] = queries
        score = lax.dot_general(keys, queries, (((0,), (0,)), ((), ())), preferred_element_type=F32)
        score = jnp.where(visible, score * FACTOR, MASK_FILL)
        top = jnp.max(score, 0, keepdims=True)
        exponent = jnp.exp(score - top)
        total = jnp.sum(exponent, 0, keepdims=True)
        prob = (exponent * (1.0 / total)).astype(BF16)
        attended[at, :] = jnp.dot(values, prob, preferred_element_type=F32).astype(BF16)
        log_total[0, h : h + 1, :] = top + jnp.log(total)


def attention_back_kernel(
    heads, rotated, grad_att, log_total, cosine, sine, owner_col, owner_row, grad_qkv
):
    cos, sin = cosine[...], sine[...]
    width = heads * HEAD_SIZE
    visible = visible_block(owner_col[0], owner_row[0])
    keys = rotated[width : width + HEAD_SIZE, :]
    values = rotated[width + HEAD_SIZE :, :]
    length = keys.shape[1]
    grad_keys = jnp.zeros((HEAD_SIZE, length), F32)
    grad_values = jnp.zeros((HEAD_SIZE, length), F32)
    for h in range(heads):
        at = slice(h * HEAD_SIZE, (h + 1) * HEAD_SIZE)
        queries = rotated[at, :]
        grad = grad_att[at, :]
        score = lax.dot_general(keys, queries, (((0,), (0,)), ((), ())), preferred_element_type=F32)
        score = jnp.where(visible, score * FACTOR, MASK_FILL)
        prob = jnp.exp(score - log_total[0, h : h + 1, :])
        grad_prob = lax.dot_general(
            values, grad, (((0,), (0,)), ((), ())), preferred_element_type=F32
        )
        inner = jnp.sum(prob * grad_prob, 0, keepdims=True)
        grad_score = (FACTOR * prob * (grad_prob - inner)).astype(BF16)
        grad_query = jnp.dot(keys, grad_score, preferred_element_type=F32)
        grad_qkv[at, :] = rope_back(grad_query, cos, sin).astype(BF16)
        grad_keys += lax.dot_general(
            queries, grad_score, (((1,), (1,)), ((), ())), preferred_element_type=F32
        )
        grad_values += lax.dot_general(
            grad, prob.astype(BF16), (((1,), (1,)), ((), ())), preferred_element_type=F32
        )
    grad_qkv[width : width + HEAD_SIZE, :] = rope_back(grad_keys, cos, sin).astype(BF16)
    grad_qkv[width + HEAD_SIZE :, :] = grad_values.astype(BF16)


def attention_specs(heads, length):
    rows = (heads + 2) * HEAD_SIZE
    whole = lambda height: pl.BlockSpec((height, length), lambda i: (0, i))
    table = pl.BlockSpec((HEAD_SIZE, length), lambda i: (0, 0))
    logs = pl.BlockSpec((1, heads, length), lambda i: (i, 0, 0))
    col = pl.BlockSpec((1, length, 1), lambda i: (i, 0, 0))
    row = pl.BlockSpec((1, 1, length), lambda i: (i, 0, 0))
    return whole(rows), whole(heads * HEAD_SIZE), logs, table, col, row


def attention(qkv, owners, tables):
    count, length = owners.shape
    heads = qkv.shape[0] // HEAD_SIZE - 2
    all_spec, head_spec, logs, table, col, row = attention_specs(heads, length)
    return pl.pallas_call(
        functools.partial(attention_kernel, heads),
        grid=(count,),
        out_shape=(
            jax.ShapeDtypeStruct(qkv.shape, BF16),
            jax.ShapeDtypeStruct((heads * HEAD_SIZE, qkv.shape[1]), BF16),
            jax.ShapeDtypeStruct((count, heads, length), F32),
        ),
        in_specs=[all_spec, table, table, col, row],
        out_specs=(all_spec, head_spec, logs),
        compiler_params=pltpu.CompilerParams(vmem_limit_bytes=32 * 1024 * 1024),
    )(qkv, *tables, owners[:, :, None], owners[:, None, :])


def attention_back(rotated, grad_att, log_total, owners, tables):
    count, length = owners.shape
    heads = rotated.shape[0] // HEAD_SIZE - 2
    all_spec, head_spec, logs, table, col, row = attention_specs(heads, length)
    return pl.pallas_call(
        functools.partial(attention_back_kernel, heads),
        grid=(count,),
        out_shape=jax.ShapeDtypeStruct(rotated.shape, BF16),
        in_specs=[all_spec, head_spec, logs, table, table, col, row],
        out_specs=all_spec,
        compiler_params=pltpu.CompilerParams(vmem_limit_bytes=32 * 1024 * 1024),
    )(rotated, grad_att, log_total, *tables, owners[:, :, None], owners[:, None, :])


def contract(left, right, left_dim, right_dim, kind=F32):
    return lax.dot_general(
        left, right, (((left_dim,), (right_dim,)), ((), ())), preferred_element_type=F32
    ).astype(kind)


def normed(values, gain):
    inverse = lax.rsqrt(jnp.mean(values * values, -1, keepdims=True) + NORM_EPSILON)
    return (values * inverse * gain).astype(BF16)


def norm_back(grad, values, gain):
    inverse = lax.rsqrt(jnp.mean(values * values, -1, keepdims=True) + NORM_EPSILON)
    scaled = values * inverse
    gained = grad * gain
    into = inverse * (gained - scaled * jnp.mean(gained * scaled, -1, keepdims=True))
    return into, jnp.sum(grad * scaled, 0, keepdims=True)


def reordered(values):
    count = lax.axis_size("dp")
    width = values.shape[-1]
    parts = values.reshape(values.shape[:-1] + (count, width // count))
    axis = parts.ndim - 2
    for _, bit in dp_bits():
        low = [lax.slice_in_dim(parts, i ^ (1 << bit), (i ^ (1 << bit)) + 1, axis=axis) for i in range(count)]
        parts = jnp.where(side(("dp", bit)) == 1, jnp.concatenate(low, axis), parts)
    return parts.reshape(values.shape)


class Wires:
    def __init__(self, send, recv):
        self.send, self.recv, self.count, self.started = send, recv, 0, []
        self.index = {name: lax.axis_index(name) for name in ("section", "dp", "tensor")}

    def partner(self, place):
        axis, bit = place
        where = dict(self.index)
        low = lax.rem(where[axis] // (1 << bit), 2)
        where[axis] = where[axis] + (1 - 2 * low) * (1 << bit)
        return (where["section"], where["dp"], where["tensor"])

    def go(self, source, target, place):
        copy = pltpu.make_async_remote_copy(
            src_ref=source,
            dst_ref=target,
            send_sem=self.send.at[self.count],
            recv_sem=self.recv.at[self.count],
            device_id=self.partner(place),
            device_id_type=pl.DeviceIdType.MESH,
        )
        self.count += 1
        copy.start()
        self.started.append(copy)
        return copy

    def drain(self):
        for copy in self.started:
            copy.wait_send()


def crossed(values, group):
    count = values.shape[-1] // group
    return jnp.concatenate(
        [values[:, (g ^ 1) * group : ((g ^ 1) + 1) * group] for g in range(count)], 1
    )


def exchange_kernel(rs, ag, middle, n_in, n_out, group, *refs):
    refs = list(refs)
    take = lambda count: [refs.pop(0) for _ in range(count)]
    partial = take(1)[0] if rs else None
    ins = take(n_in)
    gathered = take(1)[0] if ag else None
    outs = take(n_out)
    send, recv, local = take(3)
    wires = Wires(send, recv)
    section, tensor = wires.index["section"], wires.index["tensor"]
    places = [TENSOR, SECTION] + ([SHARED] if 8 in (rs, ag) else [])
    barrier = pltpu.get_barrier_semaphore()
    for place in places:
        pl.semaphore_signal(
            barrier, inc=1, device_id=wires.partner(place), device_id_type=pl.DeviceIdType.MESH
        )
    pl.semaphore_wait(barrier, len(places))
    total = None
    if rs == 8:
        mine, core, out, from_y, from_z, part_y, part_z = take(7)
        half = mine.shape[1] // 2
        lo, hi = pl.ds(0, half), pl.ds(half, half)
        near, far = {}, {}
        for c in (3, 1, 2, 0):
            near[c] = pltpu.make_async_copy(partial.at[2 * c], mine.at[c], local.at[c])
            near[c].start()
            far[c] = wires.go(partial.at[2 * c + 1], core.at[c], TENSOR)

        def ready(c):
            near[c].wait()
            far[c].wait_recv()

        def added(c, rows):
            return mine[c, rows, :].astype(F32) + core[c, rows, :].astype(F32)

        ready(3)
        out[2, lo, :] = added(3, lo).astype(BF16)
        diag_y = wires.go(out.at[2, lo], part_y, SECTION)
        out[2, hi, :] = crossed(added(3, hi), group).astype(BF16)
        diag_z = wires.go(out.at[2, hi], part_z, SHARED)
        ready(1)
        out[0, lo, :] = added(1, lo).astype(BF16)
        first_y = wires.go(out.at[0, lo], from_y.at[lo], SECTION)
        ready(2)
        out[1, hi, :] = crossed(added(2, hi), group).astype(BF16)
        first_z = wires.go(out.at[1, hi], from_z.at[hi], SHARED)
        diag_y.wait_recv()
        out[1, lo, :] = crossed(added(2, lo) + part_y[...].astype(F32), group).astype(BF16)
        second_z = wires.go(out.at[1, lo], from_z.at[lo], SHARED)
        diag_z.wait_recv()
        out[0, hi, :] = (added(1, hi) + part_z[...].astype(F32)).astype(BF16)
        second_y = wires.go(out.at[0, hi], from_y.at[hi], SECTION)
        ready(0)
        for copy in (first_y, second_y, first_z, second_z):
            copy.wait_recv()
        total = (
            mine[0].astype(F32) + core[0].astype(F32) + from_y[...].astype(F32) + from_z[...].astype(F32)
        )
    elif rs == 4:
        mine, core, out, from_y = take(4)
        near, far = {}, {}
        for c in (1, 0):
            slot = 2 * (section + c - 2 * c * section)
            near[c] = pltpu.make_async_copy(partial.at[slot + tensor], mine.at[c], local.at[c])
            near[c].start()
            far[c] = wires.go(partial.at[slot + 1 - tensor], core.at[c], TENSOR)
        near[1].wait()
        far[1].wait_recv()
        out[...] = (mine[1].astype(F32) + core[1].astype(F32)).astype(BF16)
        over_y = wires.go(out, from_y, SECTION)
        near[0].wait()
        far[0].wait_recv()
        over_y.wait_recv()
        total = mine[0].astype(F32) + core[0].astype(F32) + from_y[...].astype(F32)
    rows = middle(total, ins, outs)
    if ag:
        own = take(1)[0]
        own[...] = rows
        half = own.shape[0] // 2
        lo, hi = pl.ds(0, half), pl.ds(half, half)
    if ag == 8:
        turned = take(1)[0]
        turned[...] = crossed(rows, group)
        over_y_hi = wires.go(own.at[hi], gathered.at[2, hi], SECTION)
        over_z_lo = wires.go(turned.at[lo], gathered.at[4, lo], SHARED)
        over_y_lo = wires.go(own.at[lo], gathered.at[2, lo], SECTION)
        over_z_hi = wires.go(turned.at[hi], gathered.at[4, hi], SHARED)
        over_core = [wires.go(own, gathered.at[1], TENSOR)]
        keep = pltpu.make_async_copy(own, gathered.at[0], local.at[4])
        keep.start()
        diag = []
        over_y_hi.wait_recv()
        for g in range(own.shape[1] // group):
            diag.append(
                wires.go(
                    gathered.at[2, hi, pl.ds(g * group, group)],
                    gathered.at[6, hi, pl.ds((g ^ 1) * group, group)],
                    SHARED,
                )
            )
        over_z_lo.wait_recv()
        diag.append(wires.go(gathered.at[4, lo], gathered.at[6, lo], SECTION))
        over_y_lo.wait_recv()
        over_core.append(wires.go(gathered.at[2], gathered.at[3], TENSOR))
        over_z_hi.wait_recv()
        over_core.append(wires.go(gathered.at[4], gathered.at[5], TENSOR))
        for copy in diag:
            copy.wait_recv()
        over_core.append(wires.go(gathered.at[6], gathered.at[7], TENSOR))
        for copy in over_core:
            copy.wait_recv()
        keep.wait()
    elif ag == 4:
        slot = 2 * section + tensor
        across = 2 * (1 - section) + tensor
        over_y = wires.go(own, gathered.at[slot], SECTION)
        over_core = [wires.go(own, gathered.at[slot], TENSOR)]
        keep = pltpu.make_async_copy(own, gathered.at[slot], local.at[4])
        keep.start()
        over_y.wait_recv()
        over_core.append(wires.go(gathered.at[across], gathered.at[across], TENSOR))
        for copy in over_core:
            copy.wait_recv()
        keep.wait()
    wires.drain()


def exchange(rs, ag, middle, partial, ins, outs, collective_id):
    rows, width = 0, 0
    if rs:
        rows, width = partial.shape[0] // rs, partial.shape[1]
        partial = partial.reshape(rs, rows, width)
    else:
        rows, width = ins[0].shape
    group = 2 * width // lax.axis_size("dp")
    block = lambda *lead: pltpu.VMEM(lead + (rows, width), BF16)
    anywhere = pl.BlockSpec(memory_space=pl.ANY)
    inside = pl.BlockSpec(memory_space=pltpu.VMEM)
    wires = 16 + 2 * (width // group)
    scratch = [
        pltpu.SemaphoreType.DMA((wires,)),
        pltpu.SemaphoreType.DMA((wires,)),
        pltpu.SemaphoreType.DMA((5,)),
    ]
    if rs == 8:
        part = pltpu.VMEM((rows // 2, width), BF16)
        scratch += [block(4), block(4), block(3), block(), block(), part, part]
    elif rs == 4:
        scratch += [block(2), block(2), block(), block()]
    if ag:
        scratch += [block()]
    if ag == 8:
        scratch += [block()]
    out_shape = ([jax.ShapeDtypeStruct((ag, rows, width), BF16)] if ag else []) + list(outs)
    results = pl.pallas_call(
        functools.partial(exchange_kernel, rs, ag, middle, len(ins), len(outs), group),
        out_shape=out_shape,
        in_specs=([anywhere] if rs else []) + [inside] * len(ins),
        out_specs=([anywhere] if ag else []) + [inside] * len(outs),
        scratch_shapes=scratch,
        compiler_params=pltpu.CompilerParams(
            collective_id=collective_id, has_side_effects=True, vmem_limit_bytes=40 * 1024 * 1024
        ),
    )(*(([partial] if rs else []) + list(ins)))
    results = list(results)
    if ag:
        results[0] = results[0].reshape(ag * rows, width)
    return results


def start_rows(total, ins, outs):
    return normed(ins[0][...], ins[1][...])


def bare_rows(total, ins, outs):
    return ins[0][...]


def forward_rows(total, ins, outs):
    middle = ins[0][...] + total
    outs[0][...] = middle
    return normed(middle, ins[1][...])


def handed_rows(total, ins, outs):
    handed = (ins[0][...] + total).astype(BF16).astype(F32)
    outs[0][...] = handed
    return normed(handed, ins[1][...])


def last_rows(total, ins, outs):
    outs[0][...] = (ins[0][...] + total).astype(BF16)


def back_rows(total, ins, outs):
    through, values, gain = ins
    into, term = norm_back(total, values[...], gain[...])
    result = through[...].astype(F32) + into
    outs[1][...] = term
    outs[0][...] = result.astype(outs[0].dtype)
    return result.astype(BF16)


def like(block, kind):
    return jax.ShapeDtypeStruct(block.shape, kind)


def mlp_forward(rows_mlp, weights):
    w_gu, w_d = weights[1:]
    gate_up = contract(rows_mlp, w_gu, 1, 0)
    units = gate_up.shape[1] // 2
    gate, up = gate_up[:, :units], gate_up[:, units:]
    hidden = (gate * jax.nn.sigmoid(gate) * up).astype(BF16)
    return gate_up, hidden, contract(hidden, w_d, 1, 1, BF16)


def mlp_backward(grad_out, rows_mlp, gate_up, hidden, weights):
    w_gu, w_d = weights[1:]
    term_d = contract(grad_out, hidden, 0, 0, BF16)
    grad_hidden = contract(grad_out, w_d, 1, 0, BF16).astype(F32)
    units = gate_up.shape[1] // 2
    gate, up = gate_up[:, :units], gate_up[:, units:]
    sig = jax.nn.sigmoid(gate)
    grad_gate = grad_hidden * up * sig * (1.0 + gate * (1.0 - sig))
    grad_up = grad_hidden * (gate * sig)
    grad_gu = jnp.concatenate([grad_gate, grad_up], 1).astype(BF16)
    partial = contract(grad_gu, w_gu, 1, 1, BF16)
    return partial, term_d, contract(rows_mlp, grad_gu, 0, 0, BF16)


def attn_forward(rows_attn, weights, owners, tables):
    w_attn = weights[0]
    width = w_attn.shape[1] - attn_split(w_attn)
    qkv = contract(w_attn[:, : attn_split(w_attn)], rows_attn, 0, 1)
    rotated, attended, log_total = attention(qkv, owners, tables)
    return rotated, attended, log_total, contract(attended, w_attn[:, attn_split(w_attn) :], 0, 1, BF16)


def attn_split(w_attn):
    return (w_attn.shape[1] - 2 * HEAD_SIZE) // 2 + 2 * HEAD_SIZE


def attn_backward(grad_branch, rows_attn, rotated, attended, log_total, weights, owners, tables):
    w_attn = weights[0]
    at = attn_split(w_attn)
    grad_att = contract(w_attn[:, at:], grad_branch, 0, 1, BF16)
    grad_qkv = attention_back(rotated, grad_att, log_total, owners, tables)
    partial = contract(grad_qkv, w_attn[:, :at], 0, 1, BF16)
    term_o = contract(grad_branch, attended, 0, 1, BF16)
    term_qkv = contract(rows_attn, grad_qkv, 0, 1, BF16)
    return partial, jnp.concatenate([term_qkv, term_o], 1)


X_BIT = ("dp", 0)


class Hops(Wires):
    def __init__(self, send, recv):
        super().__init__(send, recv)
        self.other = 1 - self.index["section"]

    def to(self, offset):
        dp = self.index["dp"]
        for bit in range(offset.bit_length()):
            if offset >> bit & 1:
                low = lax.rem(dp // (1 << bit), 2)
                dp = dp + (1 - 2 * low) * (1 << bit)
        return (self.index["section"], dp, self.index["tensor"])

    def across(self):
        return (self.other, self.index["dp"], self.index["tensor"])

    def make(self, source, target, device):
        copy = pltpu.make_async_remote_copy(
            src_ref=source,
            dst_ref=target,
            send_sem=self.send.at[self.count],
            recv_sem=self.recv.at[self.count],
            device_id=device,
            device_id_type=pl.DeviceIdType.MESH,
        )
        return copy

    def start(self, source, target, device):
        copy = self.make(source, target, device)
        self.count += 1
        copy.start()
        self.started.append(copy)
        return copy

    def start_either(self, choice, first, second, target, device):
        copy = self.make(first, target, device)
        backup = self.make(second, target, device)
        self.count += 1
        pl.when(choice)(copy.start)
        pl.when(jnp.logical_not(choice))(backup.start)
        self.started.append(copy)
        return copy

    def greet(self, offsets):
        barrier = pltpu.get_barrier_semaphore()
        devices = [self.to(offset) for offset in offsets] + [self.across()]
        for device in devices:
            pl.semaphore_signal(
                barrier, inc=1, device_id=device, device_id_type=pl.DeviceIdType.MESH
            )
        pl.semaphore_wait(barrier, len(devices))


def reached(count):
    return [1] + [2 * k for k in range(1, count // 2)]


def gather_kernel(count, *refs):
    packs, crossed_over, full = refs[:3], refs[3:6], (refs[6:9], refs[9:12])
    send, recv, local = refs[12:]
    hops = Hops(send, recv)
    section = hops.index["section"]
    half = lax.rem(hops.index["dp"] // 2, 2)
    kinds = count // 2
    hops.greet(reached(count))
    keeps = []
    over = [
        hops.start(packs[a].at[hops.other], crossed_over[a], hops.across()) for a in range(3)
    ]

    def source(a, layer, other):
        if a == 0:
            return packs[0].at[section], crossed_over[0]
        which = 1 - half if other else half
        return packs[a].at[section, which], crossed_over[a].at[which]

    def from_source(a, layer, other, target, device):
        first, second = source(a, layer, other)
        return hops.start_either(section == layer, first, second, target, device)

    arrived = {}

    def begin(a, layer):
        out = full[layer][a]
        first, second = source(a, layer, False)
        keep = pltpu.make_async_copy(first, out.at[0], local.at[3 * layer + a])
        backup = pltpu.make_async_copy(second, out.at[0], local.at[3 * layer + a])
        pl.when(section == layer)(keep.start)
        pl.when(section != layer)(backup.start)
        keeps.append(keep)
        for k in reversed(range(1, kinds)):
            if a > 0 or k == 1 or k % 2 == 0:
                arrived[a, layer, k] = from_source(
                    a, layer, k % 2 == 1, out.at[2 * k], hops.to(2 * k)
                )
        arrived[a, layer, "x0"] = from_source(a, layer, False, out.at[1], hops.to(1))

    def onward(a, layer):
        out = full[layer][a]
        for k in reversed(range(1, kinds)):
            if a > 0 or k == 1 or k % 2 == 0:
                arrived[a, layer, k].wait_recv()
                arrived[a, layer, "x", k] = hops.start(out.at[2 * k], out.at[2 * k + 1], hops.to(1))
                if a == 0 and k % 2 == 0:
                    arrived[a, layer, k + 1] = hops.start(
                        out.at[2 * k], out.at[2 * k + 2], hops.to(2)
                    )

    def finish(a, layer):
        out = full[layer][a]
        if a == 0:
            for k in reversed(range(2, kinds, 2)):
                arrived[a, layer, "x", k].wait_recv()
                arrived[a, layer, "x", k + 1] = hops.start(
                    out.at[2 * k + 1], out.at[2 * k + 3], hops.to(2)
                )

    order = [(0, 0), (1, 0), (2, 0), (0, 1), (1, 1), (2, 1)]
    for place, (a, layer) in enumerate(order):
        if layer == 0:
            over[a].wait_recv()
        begin(a, layer)
        if place:
            onward(*order[place - 1])
        if place > 1:
            finish(*order[place - 2])
    onward(*order[-1])
    finish(*order[-2])
    finish(*order[-1])
    for a, layer in order:
        arrived[a, layer, "x0"].wait_recv()
        for k in range(1, kinds):
            if a == 0 and k % 2 == 1 and k > 1:
                arrived[a, layer, k].wait_recv()
            if a > 0 or k % 2 == 1:
                arrived[a, layer, "x", k].wait_recv()
    for keep in keeps:
        keep.wait()
    hops.drain()


def gathered_weights(packs):
    count = lax.axis_size("dp")
    anywhere = pl.BlockSpec(memory_space=pl.ANY)
    rows = packs[0].shape[-2]
    over = [jax.ShapeDtypeStruct(pack.shape[1:], BF16) for pack in packs]
    full = [jax.ShapeDtypeStruct((count, rows, pack.shape[-1]), BF16) for pack in packs]
    wires = 3 + 6 * (count - 1)
    results = pl.pallas_call(
        functools.partial(gather_kernel, count),
        out_shape=over + full + full,
        in_specs=[anywhere] * 3,
        out_specs=[anywhere] * 9,
        scratch_shapes=[
            pltpu.SemaphoreType.DMA((wires,)),
            pltpu.SemaphoreType.DMA((wires,)),
            pltpu.SemaphoreType.DMA((6,)),
        ],
        compiler_params=pltpu.CompilerParams(collective_id=10, has_side_effects=True),
    )(*packs)
    flat = [block.reshape(-1, block.shape[-1]) for block in results[3:]]
    return flat[:3], flat[3:]


CHUNK = 32


def scatter_kernel(count, rows, *refs):
    terms, outs = (refs[:3], refs[3:6]), refs[6:9]
    send, recv, local = refs[9:12]
    landed, loaded = (refs[12:15], refs[15:18]), (refs[18:21], refs[21:24])
    distant = (refs[24:27], refs[27:30])
    hops = Hops(send, recv)
    section = hops.index["section"]
    half = lax.rem(hops.index["dp"] // 2, 2)
    kinds = count // 2
    hops.greet(reached(count))
    chunk = min(CHUNK, rows)

    def add(target, sources):
        @pl.loop(0, rows // chunk)
        def _(i):
            at = pl.ds(pl.multiple_of(i * chunk, chunk), chunk)
            total = sources[0][at, :].astype(F32)
            for source in sources[1:]:
                total = total + source[at, :].astype(F32)
            target[at, :] = total.astype(BF16)

    copies, loads = {}, {}
    used = [0]

    def load(a, layer, r):
        copy = pltpu.make_async_copy(
            terms[layer][a].at[r], loaded[layer][a].at[r // 2], local.at[used[0]]
        )
        used[0] += 1
        copy.start()
        return copy

    def begin(a, layer):
        term, land = terms[layer][a], landed[layer][a]
        for k in reversed(range(kinds)):
            if a > 0 or k < 2 or k % 2 == 0:
                loads[a, layer, k] = load(a, layer, 2 * k)
        if a == 0:
            for k in range(2, kinds, 2):
                for j in (1, 0):
                    copies[a, layer, "s", k + j] = hops.start(
                        term.at[2 * k + 2 + j], land.at[kinds + k + j], hops.to(2)
                    )
                copy = pltpu.make_async_copy(
                    term.at[2 * k + 1], loaded[layer][a].at[k + 1], local.at[used[0]]
                )
                used[0] += 1
                copy.start()
                loads[a, layer, "x", k] = copy
        for k in reversed(range(kinds)):
            if a > 0 or k < 2:
                copies[a, layer, "x", k] = hops.start(term.at[2 * k + 1], land.at[k], hops.to(1))

    def shared_first(a, layer):
        if a:
            return
        land, kept = landed[layer][a], loaded[layer][a]
        for k in range(2, kinds, 2):
            copies[a, layer, "s", k + 1].wait_recv()
            loads[a, layer, "x", k].wait()
            add(kept.at[k + 1], [kept.at[k + 1], land.at[kinds + k + 1]])
            copies[a, layer, "x", k] = hops.start(kept.at[k + 1], land.at[k], hops.to(1))

    def onward(a, layer):
        land, kept = landed[layer][a], loaded[layer][a]
        for k in reversed(range(kinds)):
            if a == 0 and k > 1 and k % 2 == 1:
                continue
            loads[a, layer, k].wait()
            copies[a, layer, "x", k].wait_recv()
            parts = [kept.at[k], land.at[k]]
            if a == 0 and k > 1:
                copies[a, layer, "s", k].wait_recv()
                parts.append(land.at[kinds + k])
            add(kept.at[k], parts)
            if k:
                copies[a, layer, "z", k] = hops.start(
                    kept.at[k], distant[layer][a].at[k - 1], hops.to(2 * k)
                )

    ending = []

    def finish(a, layer):
        kept, far = loaded[layer][a], distant[layer][a]
        result = landed[layer][a]
        mine, other = [kept.at[0]], []
        for k in range(1, kinds):
            if (a, layer, "z", k) in copies:
                copies[a, layer, "z", k].wait_recv()
                (other if a and k % 2 else mine).append(far.at[k - 1])
        if a:
            add(result.at[0], mine)
            add(result.at[1], other)
            pieces = [(result.at[0], half), (result.at[1], 1 - half)]
        else:
            add(result.at[0], mine)
            pieces = [(result.at[0], None)]
        for piece, which in pieces:
            target = outs[a].at[section] if which is None else outs[a].at[section, which]
            index = used[0]
            used[0] += 1
            keep = pltpu.make_async_copy(piece, target, local.at[index])
            away = hops.make(piece, target, hops.across())
            hops.count += 1
            pl.when(section == layer)(keep.start)
            pl.when(section != layer)(away.start)
            ending.append((layer, keep, away))

    order = [(2, 1), (1, 1), (0, 1), (2, 0), (1, 0), (0, 0)]
    for place, (a, layer) in enumerate(order):
        begin(a, layer)
        if place:
            onward(*order[place - 1])
        shared_first(a, layer)
        if place > 1:
            finish(*order[place - 2])
    onward(*order[-1])
    finish(*order[-2])
    finish(*order[-1])
    for layer, keep, away in ending:
        @pl.when(section == layer)
        def _():
            keep.wait()
            away.wait_recv()

        pl.when(section != layer)(away.wait_send)
    hops.drain()


def scattered_terms(terms, rows):
    count = lax.axis_size("dp")
    kinds = count // 2
    anywhere = pl.BlockSpec(memory_space=pl.ANY)
    flat = [term.reshape(count, rows, term.shape[1]) for term in terms[0] + terms[1]]
    columns = [term.shape[1] for term in terms[0]]
    outs = [
        jax.ShapeDtypeStruct((2, rows, columns[0]), BF16),
        jax.ShapeDtypeStruct((2, 2, rows, columns[1]), BF16),
        jax.ShapeDtypeStruct((2, 2, rows, columns[2]), BF16),
    ]
    wires = 12 + 6 * (count + kinds)
    block = lambda depth, a: pltpu.VMEM((depth, rows, columns[a]), BF16)
    landed = [block(2 * kinds if a == 0 else kinds, a) for a in range(3)]
    loaded = [block(kinds, a) for a in range(3)]
    distant = [block(kinds - 1, a) for a in range(3)]
    return pl.pallas_call(
        functools.partial(scatter_kernel, count, rows),
        out_shape=outs,
        in_specs=[anywhere] * 6,
        out_specs=[anywhere] * 3,
        scratch_shapes=[
            pltpu.SemaphoreType.DMA((wires,)),
            pltpu.SemaphoreType.DMA((wires,)),
            pltpu.SemaphoreType.DMA((wires,)),
        ]
        + landed
        + landed
        + loaded
        + loaded
        + distant
        + distant,
        compiler_params=pltpu.CompilerParams(
            collective_id=11, has_side_effects=True, vmem_limit_bytes=58 * 1024 * 1024
        ),
    )(*flat)


def halves(block, axis):
    shape = block.shape
    return block.reshape(shape[:axis] + (2, shape[axis] // 2) + shape[axis + 1 :])


def shards(
    layer_in,
    out_grad,
    doc_lengths,
    attn_gain,
    w_query,
    keyval_weight,
    w_out,
    mlp_gain,
    w_gate_up,
    w_down,
):
    section = lax.axis_index("section")
    first = section == 0
    micro, seqs, here, columns = layer_in.shape
    length = here * lax.axis_size("tensor")
    rows = w_query.shape[1]

    def whole_rows(block):
        kept = pick(block, section, 0)
        other = swap(pick(block, 1 - section, 0), SECTION)
        joined = pair(kept, other, SECTION, 2)
        return reordered(joined.reshape(seqs * here, 2 * columns))

    gain_block = jnp.concatenate([attn_gain, mlp_gain], 0)
    gains_both = reordered(pair(gain_block, swap(gain_block, SECTION), SECTION, 0))
    attn_gains = [gains_both[layer, 0][None] for layer in range(2)]
    mlp_gains = [gains_both[layer, 1][None] for layer in range(2)]
    entering = whole_rows(layer_in).astype(F32)
    cotangent = whole_rows(out_grad)

    q = halves(w_query[0], 1)
    kv = halves(keyval_weight[0], 2).swapaxes(1, 2).reshape(rows, 2, -1)
    pack_attn = jnp.concatenate([q, kv, halves(w_out[0], 1)], 2).swapaxes(0, 1)
    pack_gu = halves(halves(w_gate_up[0], 2), 3).transpose(2, 3, 0, 1, 4).reshape(2, 2, rows, -1)
    pack_d = halves(halves(w_down[0], 1), 2).transpose(1, 2, 0, 3)
    weights = gathered_weights([pack_attn, pack_gu, pack_d])
    owners = owners_of(doc_lengths.reshape(micro * seqs, -1), length)
    tables = rope_tables(length)
    gain_like = jax.ShapeDtypeStruct((1, entering.shape[1]), F32)

    entered, middles, saved = [], [], []
    (rows_attn,) = exchange(0, 4, start_rows, None, [entering, attn_gains[0]], [], 0)
    for layer in range(2):
        entered.append(entering)
        rotated, attended, log_total, partial = attn_forward(
            rows_attn, weights[layer], owners, tables
        )
        rows_mlp, middle = exchange(
            4,
            8,
            forward_rows,
            partial,
            [entering, mlp_gains[layer]],
            [like(entering, F32)],
            1 + 2 * layer,
        )
        middles.append(middle)
        gate_up, hidden, partial = mlp_forward(rows_mlp, weights[layer])
        saved.append((rows_attn, rotated, attended, log_total, rows_mlp, gate_up, hidden))
        if layer == 0:
            rows_attn, entering = exchange(
                8, 4, handed_rows, partial, [middle, attn_gains[1]], [like(entering, F32)], 2
            )
        else:
            (last,) = exchange(8, 0, last_rows, partial, [middle], [like(entering, BF16)], 4)
    (grad_out,) = exchange(0, 8, bare_rows, None, [cotangent], [], 5)
    through = cotangent
    terms, gain_terms = [None, None], [None, None]
    for layer in (1, 0):
        rows_attn, rotated, attended, log_total, rows_mlp, gate_up, hidden = saved[layer]
        partial, term_d, term_gu = mlp_backward(grad_out, rows_mlp, gate_up, hidden, weights[layer])
        grad_branch, grad_middle, mlp_term = exchange(
            8,
            4,
            back_rows,
            partial,
            [through, middles[layer], mlp_gains[layer]],
            [like(entering, F32), gain_like],
            9 - 3 * layer,
        )
        partial, term_attn = attn_backward(
            grad_branch, rows_attn, rotated, attended, log_total, weights[layer], owners, tables
        )
        back = [grad_middle, entered[layer], attn_gains[layer]]
        if layer == 1:
            grad_out, through, attn_term = exchange(
                4, 8, back_rows, partial, back, [like(entering, BF16), gain_like], 7
            )
        else:
            through, attn_term = exchange(
                4, 0, back_rows, partial, back, [like(entering, BF16), gain_like], 8
            )
        terms[layer] = (term_attn, term_gu, term_d)
        gain_terms[layer] = jnp.concatenate([attn_term, mlp_term], 0)

    sum_attn, sum_gu, sum_d = scattered_terms(terms, rows)
    query_half = w_query.shape[2] // 2
    kv_half = keyval_weight.shape[3]
    grad_attn = sum_attn.astype(F32).swapaxes(0, 1)
    grad_q = grad_attn[:, :, :query_half].reshape(w_query.shape)
    grad_kv = grad_attn[:, :, query_half : query_half + kv_half].reshape(rows, 2, 2, -1).swapaxes(1, 2)
    grad_o = grad_attn[:, :, query_half + kv_half :].reshape(w_out.shape)
    grad_gu = sum_gu.astype(F32).reshape(2, 2, rows, 2, -1).transpose(2, 3, 0, 1, 4)
    grad_d = sum_d.astype(F32).transpose(2, 0, 1, 3)

    gain_sum = reordered(jnp.stack(gain_terms))
    for place in [TENSOR, SECTION] + dp_bits():
        gain_sum = gain_sum + swap(gain_sum, place)
    own_gains = pick(gain_sum, section, 0)

    def half_columns(block):
        parts = reordered(block).reshape(seqs, here, 2, columns)
        kept = pick(parts, section, 2)
        other = swap(pick(parts, 1 - section, 2), SECTION)
        return pair(kept, other, SECTION, 0)

    layer_out = half_columns(last)
    in_grad = half_columns(through)
    return (
        layer_out,
        in_grad,
        own_gains[0][None],
        grad_q,
        grad_kv.reshape(keyval_weight.shape),
        grad_o,
        own_gains[1][None],
        grad_gu.reshape(w_gate_up.shape),
        grad_d.reshape(w_down.shape),
    )


def solution(mesh):
    activation = P(None, "dp", "tensor", "section")
    matrix = P("section", "dp", "tensor")
    stacked = P("section", "dp", None, "tensor")
    gain = P("section", None)
    return jax.shard_map(
        shards,
        mesh=mesh,
        in_specs=(
            activation,
            activation,
            P(None, "dp", None),
            gain,
            matrix,
            stacked,
            matrix,
            gain,
            stacked,
            matrix,
        ),
        out_specs=(
            activation,
            activation,
            gain,
            matrix,
            stacked,
            matrix,
            gain,
            stacked,
            matrix,
        ),
        check_vma=False,
    )
```

time: 3720 us -> 1240 us (0.33)
  waiting for transfers between devices: 3070 us -> 1.99 us
  Pallas kernels: 0 us -> 961 us
  matrix products: 369 us -> 115 us
  other arithmetic: 111 us -> 25.8 us
  blocking collectives: 64.6 us -> 0 us
  local copies, waits for them, and re-layouts: 63.3 us -> 110 us
    reduce_scatter x24 -> x0, waiting for transfers between devices: 2170 us -> none  [the longest x12 2110 us: weight_term(): lax.psum_scatter(lax.dot_general(left_rows, right_rows, (((0,), (0,)), ((...]
    pallas_call x0 -> x16, Pallas kernels: none -> 961 us  [the longest x1 317 us: scattered_terms(): pl.pallas_call(functools.partial(scatter_kernel, count, rows), out_shape=...]
    all_gather x17 -> x0, waiting for transfers between devices: 832 us -> none  [the longest x1 444 us: layer_forward(): lax.all_gather(w_gate_up, 'dp', axis=0, tiled=True)]
    dot_general x60 -> x24, matrix products: 364 us -> 115 us  [contract(): lax.dot_general(left, right, (((left_dim,), (right_dim,)), ((), ())), pre...]
    psum x1 -> x0, blocking collectives: 64.6 us -> none  [shards(): gain_summed = lax.psum((gain_totals[0], gain_totals[1]), ('dp', 'tensor'))]
    ppermute x6 -> x10, waiting for transfers between devices: 60.6 us -> 1.99 us  [swap(): return lax.ppermute(block, axis, [(i, i ^ 1 << bit) for i in range(count)])]
  transfers between devices with their start and end apart: 47 -> 10, of which waited for: 36 -> 1; matrix products, arithmetic and copies ran while one was open for 8% -> 9% of each run, Pallas kernels for 0% -> 51%
where the time goes in v1:
time: 1240 us; the launch traced here: 1230 us
  Pallas kernels  961 us (78%)
  matrix products  115 us (9%)
  local copies, waits for them, and re-layouts  110 us (9%)
  other arithmetic  25.8 us (2%)
    pallas_call x1, Pallas kernels, scattered_terms(): pl.pallas_call(functools.partial(scatter_kernel, count, rows), out_shape=...  317 us
    pallas_call x1, Pallas kernels, gathered_weights(): pl.pallas_call(functools.partial(gather_kernel, count), out_shape=over +...  314 us
    pallas_call x10, Pallas kernels, exchange(): pl.pallas_call(functools.partial(exchange_kernel, rs, ag, middle, len(ins...  306 us
    dot_general x24, matrix products, contract(): lax.dot_general(left, right, (((left_dim,), (right_dim,)), ((), ())), pre...  115 us
    unnamed x152, local copies, waits for them, and re-layouts  32.4 us
  transfers between devices with their start and end apart: 10, of which 1 were waited for; matrix products, arithmetic and copies ran while one was open for 9% of the time, Pallas kernels for 51%

profile of v1, /device:TPU:0, one launch (start us, length us, event | category | flops | bytes accessed | tf_op | source)
XLA Modules:
  0.0 1227.7 jit_solution(2939704383214591042)
XLA Ops:
  20.7 8.0 copy.174
  33.4 314.1 %shard_map.169 = (bf16[256,1152]{1,0:T(8,128)(2,1)}, bf16[2,256,1408]{2,1,0:T(8,128)(2,1)}, bf16[2,256,704]{2,1,0:T(8,128)(2,1)}, bf16[8,256,1152]{2,1,0:T(8,128...) custom-call(bf16[2,256,1152]{2,1,0:T(8,128)(2,1)} %maximum_bitcast_f, ...), custom_call_target="tpu_custom_call" | custom-call | tf_op jit(solution)/shard_map/pallas_call | solution.py:655
  367.0 24.9 %shard_map.177 = bf16[8,128,2048]{2,1,0:T(8,128)(2,1)S(1)} custom-call(bf16[128,2048]{1,0:T(8,128)(2,1)S(1)} %select_select_fusion.refs_0_.refs_1_), custom_call_target="tpu_custom_call" | custom-call | tf_op jit(solution)/shard_map/pallas_call | solution.py:405
  392.0 16.5 %shard_map.170 = bf16[4,128,2048]{2,1,0:T(8,128)(2,1)S(1)} custom-call(f32[128,2048]{1,0:T(8,128)S(1)} %select_convert_fusion.refs_0_.refs_1_.refs_2_, f32[1,2048]{1,0:T(1,128)S(1)} %get-tuple-element.184.refs_1_.refs_3_), custom_call_target="tpu_custom_call" | custom-call | tf_op jit(solution)/shard_map/pallas_call | solution.py:405
  418.5 36.7 %shard_map.172 = (bf16[8,128,2048]{2,1,0:T(8,128)(2,1)S(1)}, f32[128,2048]{1,0:T(8,128)S(1)}) custom-call(bf16[4,128,2048]{2,1,0:T(8,128)(2,1)S(1)} %bitcast.208, f32[128,2048]{1,0:T(8,128)S(1)} %select_convert_fusion.refs_0_.refs_1_.refs_2_, f32[1,2048]{1,0:T(1,128)S(1)} %get-tuple-element.183.refs_2_.refs_3_), custom_call_target="tpu_custom_call" | custom-call | tf_op jit(solution)/shard_map/pallas_call | solution.py:405
  455.3 6.6 fusion.63
  469.6 37.8 %shard_map.173 = (bf16[4,128,2048]{2,1,0:T(8,128)(2,1)S(1)}, f32[128,2048]{1,0:T(8,128)S(1)}) custom-call(bf16[8,128,2048]{2,1,0:T(8,128)(2,1)S(1)} %bitcast.199, f32[128,2048]{1,0:T(8,128)S(1)} %get-tuple-element.47.refs_1_.refs_2_, f32[1,2048]{1,0:T(1,128)S(1)} %get-tuple-element.182.refs_2_.refs_3_), custom_call_target="tpu_custom_call" | custom-call | tf_op jit(solution)/shard_map/pallas_call | solution.py:405
  520.2 36.8 %shard_map.175 = (bf16[8,128,2048]{2,1,0:T(8,128)(2,1)S(1)}, f32[128,2048]{1,0:T(8,128)S(1)}) custom-call(bf16[4,128,2048]{2,1,0:T(8,128)(2,1)S(1)} %bitcast.207, f32[128,2048]{1,0:T(8,128)S(1)} %get-tuple-element.50.refs_1_.refs_2_, f32[1,2048]{1,0:T(1,128)S(1)} %get-tuple-element.181.refs_2_.refs_3_), custom_call_target="tpu_custom_call" | custom-call | tf_op jit(solution)/shard_map/pallas_call | solution.py:405
  557.0 10.7 fusion.64
  573.0 8.9 convolution_convert_fusion.3
  582.0 9.0 convolution_convert_fusion
  591.0 38.3 %shard_map.178 = (bf16[4,128,2048]{2,1,0:T(8,128)(2,1)S(1)}, f32[128,2048]{1,0:T(8,128)S(1)}, f32[1,2048]{1,0:T(1,128)S(1)}) custom-call(bf16[8,128,2048]{2,1,0:T(8,128)(2,1)S(1)} %bitcast.202, bf16[128,2048]{1,0:T(8,128)(2,1)S(1)} %select_select_fusion.refs_0_.refs_1_, f32[128,2048]{1,0:T(8,128)S(1)} %get-tuple-element.54.refs_1_.refs_2_, ...), custom_call_target="tpu_custom_call" | custom-call | tf_op jit(solution)/shard_map/pallas_call | solution.py:405
  635.0 6.4 shard_map.179
  646.3 37.3 %shard_map.180 = (bf16[8,128,2048]{2,1,0:T(8,128)(2,1)S(1)}, bf16[128,2048]{1,0:T(8,128)(2,1)S(1)}, f32[1,2048]{1,0:T(1,128)S(1)}) custom-call(bf16[4,128,2048]{2,1,0:T(8,128)(2,1)S(1)} %bitcast.209, f32[128,2048]{1,0:T(8,128)S(1)} %get-tuple-element.59.refs_1_, f32[128,2048]{1,0:T(8,128)S(1)} %get-tuple-element.50.refs_1_.refs_2_, ...), custom_call_target="tpu_custom_call" | custom-call | tf_op jit(solution)/shard_map/pallas_call | solution.py:405
  694.5 8.9 convolution_convert_fusion.2
  703.4 9.2 convolution_convert_fusion.1
  712.6 38.3 %shard_map.181 = (bf16[4,128,2048]{2,1,0:T(8,128)(2,1)S(1)}, f32[128,2048]{1,0:T(8,128)S(1)}, f32[1,2048]{1,0:T(1,128)S(1)}) custom-call(bf16[8,128,2048]{2,1,0:T(8,128)(2,1)S(1)} %bitcast.203, bf16[128,2048]{1,0:T(8,128)(2,1)S(1)} %get-tuple-element.61.refs_1_, f32[128,2048]{1,0:T(8,128)S(1)} %get-tuple-element.47.refs_1_.refs_2_, ...), custom_call_target="tpu_custom_call" | custom-call | tf_op jit(solution)/shard_map/pallas_call | solution.py:405
  766.1 17.6 %shard_map.183 = (bf16[128,2048]{1,0:T(8,128)(2,1)S(1)}, f32[1,2048]{1,0:T(1,128)S(1)}) custom-call(bf16[4,128,2048]{2,1,0:T(8,128)(2,1)S(1)} %bitcast.210, f32[128,2048]{1,0:T(8,128)S(1)} %get-tuple-element.64.refs_1_, f32[128,2048]{1,0:T(8,128)S(1)} %select_convert_fusion.refs_0_.refs_1_.refs_2_, f32[1,2048]{1,0:T(1,128)S(1)} %copy-done.2), custom_call_target="tpu_custom_call" | custom-call | tf_op jit(solution)/shard_map/pallas_call | solution.py:405
  785.2 7.7 convolution_convert_fusion.6
  796.6 22.2 %shard_map.176 = bf16[128,2048]{1,0:T(8,128)(2,1)S(1)} custom-call(bf16[8,128,2048]{2,1,0:T(8,128)(2,1)S(1)} %bitcast.204, f32[128,2048]{1,0:T(8,128)S(1)} %get-tuple-element.54.refs_1_.refs_2_), custom_call_target="tpu_custom_call" | custom-call | tf_op jit(solution)/shard_map/pallas_call | solution.py:405
  842.0 6.9 copy.219
  851.7 6.8 copy.217
  862.3 316.8 %shard_map.184 = (bf16[2,256,1152]{2,1,0:T(8,128)(2,1)}, bf16[2,2,256,1408]{3,2,1,0:T(8,128)(2,1)}, bf16[2,2,256,704]{3,2,1,0:T(8,128)(2,1)}) custom-call(bf16[8,256,1152]{2,1,0:T(8,128)(2,1)} %bitcast.226, bf16[8,256,1408]{2,1,0:T(8,128)(2,1)} %bitcast.243, bf16[8,256,704]{2,1,0:T(8,128)(2,1)} %bitcast.228, bf16[8,256,1152]{2,1,0:T(8,128)(2,1)} %bitcast.225, ...), custom_call_target="tpu_custom_call" | custom-call | tf_op jit(solution)/shard_map/pallas_call | solution.py:819
  1212.9 9.6 copy.233
  (321 shorter events, 188.9 us)
Async XLA Ops:
  1.5 346.1 %collective-permute-start.1 = (f32[2,2048]{1,0:T(2,128)S(1)}, f32[2,2048]{1,0:T(2,128)S(1)}, u32[]{:S(2)}, u32[]{:S(2)}) collective-permute-start(f32[2,2048]{1,0:T(2,128)S(1)} %pad_maximum_fusion.26), channel_id=1, source_target_pairs={{0,16},{16,0},{1,17},{17,1},{2,18},{18,2},{3,19},{19,3},{4,20},{20... | collective-permute-start | bytes 49160 | tf_op jit(solution)/shard_map/ppermute | solution.py:26
  7.2 340.9 %collective-permute-start = (bf16[1,128,1024]{1,2,0:T(8,128)(2,1)}, bf16[1,128,1024]{1,2,0:T(8,128)(2,1)}, u32[]{:S(2)}, u32[]{:S(2)}) collective-permute-start(bf16[1,128,1024]{1,2,0:T(8,128)(2,1)} %bitcast.14), channel_id=1, source_target_pairs={{0,16},{16,0},{1,17},{17,1},{2,18},{18,2},{3,19},{19,3},{4,20},{20... | collective-permute-start | bytes 786440 | tf_op jit(solution)/shard_map/ppermute | solution.py:26
  9.8 345.7 %collective-permute-start.3 = (bf16[1,128,1024]{1,2,0:T(8,128)(2,1)}, bf16[1,128,1024]{1,2,0:T(8,128)(2,1)}, u32[]{:S(2)}, u32[]{:S(2)}) collective-permute-start(bf16[1,128,1024]{1,2,0:T(8,128)(2,1)} %bitcast.50), channel_id=1, source_target_pairs={{0,16},{16,0},{1,17},{17,1},{2,18},{18,2},{3,19},{19,3},{4,20},{20... | collective-permute-start | bytes 786440 | tf_op jit(solution)/shard_map/ppermute | solution.py:26
  33.4 314.2 %copy-start.38 = (f32[1,2048]{1,0:T(1,128)S(1)}, f32[1,2048]{1,0:T(1,128)}, u32[]{:S(2)}) copy-start(f32[1,2048]{1,0:T(1,128)} %param.17) | copy-start | bytes 24580
  33.4 314.2 %copy-start.39 = (f32[1,2048]{1,0:T(1,128)S(1)}, f32[1,2048]{1,0:T(1,128)}, u32[]{:S(2)}) copy-start(f32[1,2048]{1,0:T(1,128)} %param.13) | copy-start | bytes 24580
  33.4 314.6 %copy-start.27 = (bf16[1,1,128,1024]{2,3,1,0:T(8,128)(2,1)S(1)}, bf16[1,1,128,1024]{2,3,1,0:T(8,128)(2,1)}, u32[]{:S(2)}) copy-start(bf16[1,1,128,1024]{2,3,1,0:T(8,128)(2,1)} %copy.179) | copy-start | bytes 786436
  348.0 44.0 %copy-start.1 = (f32[1,2048]{1,0:T(1,128)}, f32[1,2048]{1,0:T(1,128)S(1)}, u32[]{:S(2)}) copy-start(f32[1,2048]{1,0:T(1,128)S(1)} %get-tuple-element.184.refs_1_.refs_3_) | copy-start | bytes 24580
  365.7 26.2 %copy-start.15 = (bf16[128,2048]{1,0:T(8,128)(2,1)S(1)}, bf16[128,2048]{1,0:T(8,128)(2,1)}, u32[]{:S(2)}) copy-start(bf16[128,2048]{1,0:T(8,128)(2,1)} %copy.237) | copy-start | bytes 1572868
  365.7 42.8 %slice-start.5 = ((s8[4718592]{0:T(1024)(128)(4,1)}), s8[4194304]{0:T(1024)(128)(4,1)S(1)}, s32[]{:S(2)}) async-start(s8[4718592]{0:T(1024)(128)(4,1)} %bitcast.283), calls=%async_computation.5 | async-start | bytes 8388608
  367.0 41.6 %slice-start.6 = ((s8[4718592]{0:T(1024)(128)(4,1)}), s8[524288]{0:T(1024)(128)(4,1)S(1)}, s32[]{:S(2)}) async-start(s8[4718592]{0:T(1024)(128)(4,1)} %bitcast.283), calls=%async_computation.6 | async-start | bytes 1048576
  391.9 175.9 %copy-start = (bf16[8,128,2048]{2,1,0:T(8,128)(2,1)}, bf16[8,128,2048]{2,1,0:T(8,128)(2,1)S(1)}, u32[]{:S(2)}) copy-start(bf16[8,128,2048]{2,1,0:T(8,128)(2,1)S(1)} %shard_map.177) | copy-start | bytes 12582916
  415.4 39.9 %slice-start.3 = ((s8[5767168]{0:T(1024)(128)(4,1)}), s8[4194304]{0:T(1024)(128)(4,1)S(1)}, s32[]{:S(2)}) async-start(s8[5767168]{0:T(1024)(128)(4,1)} %bitcast.277), calls=%async_computation.3 | async-start | bytes 8388608
  415.4 39.9 %slice-start.4 = ((s8[5767168]{0:T(1024)(128)(4,1)}), s8[1572864]{0:T(1024)(128)(4,1)S(1)}, s32[]{:S(2)}) async-start(s8[5767168]{0:T(1024)(128)(4,1)} %bitcast.277), calls=%async_computation.4 | async-start | bytes 3145728
  641.4 42.2 %slice-start.1 = ((s8[5767168]{0:T(1024)(128)(4,1)}), s8[4194304]{0:T(1024)(128)(4,1)S(1)}, s32[]{:S(2)}) async-start(s8[5767168]{0:T(1024)(128)(4,1)} %bitcast.238), calls=%async_computation.1 | async-start | bytes 8388608
  643.3 40.3 %slice-start.2 = ((s8[5767168]{0:T(1024)(128)(4,1)}), s8[1572864]{0:T(1024)(128)(4,1)S(1)}, s32[]{:S(2)}) async-start(s8[5767168]{0:T(1024)(128)(4,1)} %bitcast.238), calls=%async_computation.2 | async-start | bytes 3145728
  694.5 56.5 %slice-start.7 = ((s8[4718592]{0:T(1024)(128)(4,1)}), s8[4194304]{0:T(1024)(128)(4,1)S(1)}, s32[]{:S(2)}) async-start(s8[4718592]{0:T(1024)(128)(4,1)} %bitcast.286), calls=%async_computation.7 | async-start | bytes 8388608
  703.4 47.6 %slice-start.8 = ((s8[4718592]{0:T(1024)(128)(4,1)}), s8[524288]{0:T(1024)(128)(4,1)S(1)}, s32[]{:S(2)}) async-start(s8[4718592]{0:T(1024)(128)(4,1)} %bitcast.286), calls=%async_computation.8 | async-start | bytes 1048576
  820.6 16.7 %collective-permute-start.5 = (f32[2,2,2048]{2,1,0:T(2,128)S(1)}, f32[2,2,2048]{2,1,0:T(2,128)S(1)}, u32[]{:S(2)}, u32[]{:S(2)}) collective-permute-start(f32[2,2,2048]{2,1,0:T(2,128)S(1)} %fusion.39), channel_id=1, source_target_pairs={{0,1},{1,0},{2,3},{3,2},{4,5},{5,4},{6,7},{7,6},{8,9},{9,8},{10,11... | collective-permute-start | bytes 98312 | tf_op jit(solution)/shard_map/ppermute | solution.py:26
  837.3 341.8 %collective-permute-start.6 = (f32[2,2,2048]{2,1,0:T(2,128)S(1)}, f32[2,2,2048]{2,1,0:T(2,128)S(1)}, u32[]{:S(2)}, u32[]{:S(2)}) collective-permute-start(f32[2,2,2048]{2,1,0:T(2,128)S(1)} %add.52), channel_id=1, source_target_pairs={{0,16},{16,0},{1,17},{17,1},{2,18},{18,2},{3,19},{19,3},{4,20},{20... | collective-permute-start | bytes 98312 | tf_op jit(solution)/shard_map/ppermute | solution.py:26
  860.3 362.8 %collective-permute-start.2 = (bf16[1,128,1024]{1,2,0:T(8,128)(2,1)}, bf16[1,128,1024]{1,2,0:T(8,128)(2,1)}, u32[]{:S(2)}, u32[]{:S(2)}) collective-permute-start(bf16[1,128,1024]{1,2,0:T(8,128)(2,1)} %copy.194), channel_id=1, source_target_pairs={{0,16},{16,0},{1,17},{17,1},{2,18},{18,2},{3,19},{19,3},{4,20},{20... | collective-permute-start | bytes 786440 | tf_op jit(solution)/shard_map/ppermute | solution.py:26
  861.4 363.8 %collective-permute-start.4 = (bf16[1,128,1024]{1,2,0:T(8,128)(2,1)}, bf16[1,128,1024]{1,2,0:T(8,128)(2,1)}, u32[]{:S(2)}, u32[]{:S(2)}) collective-permute-start(bf16[1,128,1024]{1,2,0:T(8,128)(2,1)} %copy.214), channel_id=1, source_target_pairs={{0,16},{16,0},{1,17},{17,1},{2,18},{18,2},{3,19},{19,3},{4,20},{20... | collective-permute-start | bytes 786440 | tf_op jit(solution)/shard_map/ppermute | solution.py:26
  1179.2 5.0 collective-permute-start.7
  1184.2 4.7 collective-permute-start.8
  1188.9 33.6 %collective-permute-start.9 = (f32[2,2,2048]{2,1,0:T(2,128)S(1)}, f32[2,2,2048]{2,1,0:T(2,128)S(1)}, u32[]{:S(2)}, u32[]{:S(2)}) collective-permute-start(f32[2,2,2048]{2,1,0:T(2,128)S(1)} %add.55), channel_id=1, source_target_pairs={{0,2},{2,0},{4,6},{6,4},{8,10},{10,8},{12,14},{14,12},{1,3},{3,1},... | collective-permute-start | bytes 98312 | tf_op jit(solution)/shard_map/ppermute | solution.py:26
  (42 other events, 247.9 us)

commit v2 on v0

v2 whole, which is shorter than its diff:
```python
import functools

import jax
import jax.numpy as jnp
from jax import lax
from jax.experimental import pallas as pl
from jax.experimental.pallas import tpu as pltpu
from jax.sharding import PartitionSpec as P

HEAD_SIZE = 64
NORM_EPSILON = 1e-05
ROPE_BASE = 10000.0
MASK_FILL = -1e30
FACTOR = HEAD_SIZE ** (-0.5)
BF16 = jnp.bfloat16
F32 = jnp.float32

def rope_tables(token_length):
    middle = HEAD_SIZE // 2
    frequency = ROPE_BASE ** (-(jnp.arange(middle, dtype=F32) * 2.0) / HEAD_SIZE)
    angles = frequency[:, None] * jnp.arange(token_length, dtype=F32)[None, :]
    return (
        jnp.concatenate([jnp.cos(angles), jnp.cos(angles)], 0),
        jnp.concatenate([jnp.sin(angles), jnp.sin(angles)], 0),
    )


def owners_of(lengths, token_length):
    bounds = jnp.cumsum(lengths, -1)
    places = jnp.arange(token_length, dtype=jnp.int32)
    return jnp.sum((places[None, :, None] >= bounds[:, None, :]).astype(jnp.int32), -1)


def visible_block(owner_col, owner_row):
    length = owner_col.shape[0]
    key_place = lax.broadcasted_iota(jnp.int32, (length, length), 0)
    query_place = lax.broadcasted_iota(jnp.int32, (length, length), 1)
    return (owner_col == owner_row) & (key_place <= query_place)


def rope(u, cosine, sine):
    half = HEAD_SIZE // 2
    return u * cosine + jnp.concatenate([-u[half:], u[:half]], 0) * sine


def rope_back(u, cosine, sine):
    half = HEAD_SIZE // 2
    w = u * sine
    return u * cosine + jnp.concatenate([w[half:], -w[:half]], 0)


def normed(values, gain):
    inverse = lax.rsqrt(jnp.mean(values * values, -1, keepdims=True) + NORM_EPSILON)
    return (values * inverse * gain).astype(BF16)


def norm_back(grad, values, gain):
    inverse = lax.rsqrt(jnp.mean(values * values, -1, keepdims=True) + NORM_EPSILON)
    scaled = values * inverse
    gained = grad * gain
    into = inverse * (gained - scaled * jnp.mean(gained * scaled, -1, keepdims=True))
    return into, jnp.sum(grad * scaled, 0, keepdims=True)


def crossed(values, group):
    count = values.shape[-1] // group
    return jnp.concatenate(
        [values[:, (g ^ 1) * group : ((g ^ 1) + 1) * group] for g in range(count)], 1
    )


def reordered(values, count):
    me = lax.axis_index("dp")
    group = values.shape[-1] // count
    while group < values.shape[-1]:
        values = jnp.where(lax.rem(me, 2) == 1, crossed(values, group), values)
        me, group = me // 2, group * 2
    return values


def dot_t(left, right):
    return lax.dot_general(left, right, (((1,), (1,)), ((), ())), preferred_element_type=F32)


def dot_n(left, right):
    return jnp.dot(left, right, preferred_element_type=F32)


def dot_tn(left, right):
    return lax.dot_general(left, right, (((0,), (0,)), ((), ())), preferred_element_type=F32)


class Hops:
    def __init__(self, send, recv):
        self.send, self.recv, self.count, self.started = send, recv, 0, []
        self.index = {name: lax.axis_index(name) for name in ("section", "dp", "tensor")}
        self.other = 1 - self.index["section"]

    def to(self, offset):
        dp = self.index["dp"]
        for bit in range(offset.bit_length()):
            if offset >> bit & 1:
                low = lax.rem(dp // (1 << bit), 2)
                dp = dp + (1 - 2 * low) * (1 << bit)
        return (self.index["section"], dp, self.index["tensor"])

    def across(self):
        return (self.other, self.index["dp"], self.index["tensor"])

    def core(self):
        return (self.index["section"], self.index["dp"], 1 - self.index["tensor"])

    def at(self, source, target, device, index):
        return pltpu.make_async_remote_copy(
            src_ref=source,
            dst_ref=target,
            send_sem=self.send.at[index],
            recv_sem=self.recv.at[index],
            device_id=device,
            device_id_type=pl.DeviceIdType.MESH,
        )

    def claim(self, number=1):
        self.count += number
        return self.count - number

    def start(self, source, target, device):
        copy = self.at(source, target, device, self.claim())
        copy.start()
        self.started.append(copy)
        return copy

    def start_either(self, choice, first, second, target, device):
        index = self.claim()
        copy = self.at(first, target, device, index)
        backup = self.at(second, target, device, index)
        pl.when(choice)(copy.start)
        pl.when(jnp.logical_not(choice))(backup.start)
        self.started.append(copy)
        return copy

    def sent(self, copies):
        copies = list(copies)
        for copy in copies:
            copy.wait_send()
        gone = {id(copy) for copy in copies}
        self.started = [copy for copy in self.started if id(copy) not in gone]

    def greet(self, offsets):
        barrier = pltpu.get_barrier_semaphore()
        devices = [self.to(offset) for offset in offsets] + [self.across(), self.core()]
        for device in devices:
            pl.semaphore_signal(
                barrier, inc=1, device_id=device, device_id_type=pl.DeviceIdType.MESH
            )
        pl.semaphore_wait(barrier, len(devices))

    def drain(self):
        for copy in self.started:
            copy.wait_send()


class Local:
    AT_ONCE = 6

    def __init__(self, sems):
        self.sems, self.count = sems, self.AT_ONCE

    def claim(self, number=1):
        self.count += number
        return self.count - number

    def make(self, source, target):
        return pltpu.make_async_copy(source, target, self.sems.at[self.claim()])

    def start(self, source, target):
        copy = self.make(source, target)
        copy.start()
        return copy

    def now(self, *moves):
        waits = []
        for index, move in enumerate(moves):
            make = lambda source: pltpu.make_async_copy(source, move[-1], self.sems.at[index])
            copy = make(move[-2])
            if len(move) == 2:
                copy.start()
            else:
                pl.when(move[0])(make(move[1]).start)
                pl.when(jnp.logical_not(move[0]))(copy.start)
            waits.append(copy)
        for copy in waits:
            copy.wait()


def reached(count):
    return [1] + [2 * k for k in range(1, count // 2)]


class Spread:
    def __init__(self, hops, local, own, turned, group):
        self.hops, self.local, self.own, self.turned, self.group = hops, local, own, turned, group

    def four(self, rows, slots):
        hops, own = self.hops, self.own
        section, tensor = hops.index["section"], hops.index["tensor"]
        own[...] = rows
        slot = 2 * section + tensor
        self.over_y = hops.start(own, slots.at[slot], hops.across())
        self.over_core = hops.start(own, slots.at[slot], hops.core())
        self.keep = self.local.start(own, slots.at[slot])

    def four_end(self, slots):
        hops = self.hops
        self.over_y.wait_recv()
        across = 2 * (1 - hops.index["section"]) + hops.index["tensor"]
        last = hops.start(slots.at[across], slots.at[across], hops.core())
        self.over_core.wait_recv()
        last.wait_recv()
        self.keep.wait()
        hops.sent([self.over_y, self.over_core, last])

    def halves(self):
        half = self.own.shape[0] // 2
        return pl.ds(0, half), pl.ds(half, half)

    def eight(self, rows, slots):
        hops, own, turned = self.hops, self.own, self.turned
        own[...] = rows
        turned[...] = crossed(rows, self.group)
        lo, hi = self.halves()
        y, z, core = hops.across(), hops.to(2), hops.core()
        self.over = [
            hops.start(own.at[hi], slots.at[2, hi], y),
            hops.start(turned.at[lo], slots.at[4, lo], z),
            hops.start(own.at[lo], slots.at[2, lo], y),
            hops.start(turned.at[hi], slots.at[4, hi], z),
        ]
        self.cores = [hops.start(own, slots.at[1], core)]
        self.keep = self.local.start(own, slots.at[0])

    def eight_middle(self, slots):
        hops, group = self.hops, self.group
        lo, hi = self.halves()
        self.over[0].wait_recv()
        self.diag = [
            hops.start(
                slots.at[2, hi, pl.ds(g * group, group)],
                slots.at[6, hi, pl.ds((g ^ 1) * group, group)],
                hops.to(2),
            )
            for g in range(self.own.shape[1] // group)
        ]
        self.over[1].wait_recv()
        self.diag.append(hops.start(slots.at[4, lo], slots.at[6, lo], hops.across()))

    def eight_end(self, slots):
        hops = self.hops
        core = hops.core()
        self.over[2].wait_recv()
        self.cores.append(hops.start(slots.at[2], slots.at[3], core))
        self.over[3].wait_recv()
        self.cores.append(hops.start(slots.at[4], slots.at[5], core))
        for copy in self.diag:
            copy.wait_recv()
        self.cores.append(hops.start(slots.at[6], slots.at[7], core))
        for copy in self.cores:
            copy.wait_recv()
        self.keep.wait()
        hops.sent(self.over + self.diag + self.cores)


class Sums:
    def __init__(self, hops, partial, core, out, from_y, from_z, part_y, part_z, group):
        self.hops, self.partial, self.core, self.out, self.group = hops, partial, core, out, group
        self.from_y, self.from_z, self.part_y, self.part_z = from_y, from_z, part_y, part_z

    def four(self):
        hops, core, out, from_y, partial = self.hops, self.core, self.out, self.from_y, self.partial
        section, tensor = hops.index["section"], hops.index["tensor"]
        slots = [2 * section, 2 * (1 - section)]
        far = {
            c: hops.start(partial.at[slots[c] + 1 - tensor], core.at[c], hops.core()) for c in (1, 0)
        }
        far[1].wait_recv()
        out[0] = (partial[slots[1] + tensor].astype(F32) + core[1].astype(F32)).astype(BF16)
        over_y = hops.start(out.at[0], from_y, hops.across())
        far[0].wait_recv()
        over_y.wait_recv()
        total = (
            partial[slots[0] + tensor].astype(F32) + core[0].astype(F32) + from_y[...].astype(F32)
        )
        hops.sent([far[0], far[1], over_y])
        return total

    def halves(self):
        half = self.out.shape[1] // 2
        return pl.ds(0, half), pl.ds(half, half)

    def added(self, c, rows):
        return self.partial[2 * c, rows, :].astype(F32) + self.core[c, rows, :].astype(F32)

    def eight(self):
        hops, out, group = self.hops, self.out, self.group
        lo, hi = self.halves()
        y, z = hops.across(), hops.to(2)
        self.far = {
            c: hops.start(self.partial.at[2 * c + 1], self.core.at[c], hops.core())
            for c in (3, 1, 2, 0)
        }
        self.far[3].wait_recv()
        out[2, lo, :] = self.added(3, lo).astype(BF16)
        self.diag_y = hops.start(out.at[2, lo], self.part_y, y)
        out[2, hi, :] = crossed(self.added(3, hi), group).astype(BF16)
        self.diag_z = hops.start(out.at[2, hi], self.part_z, z)
        self.far[1].wait_recv()
        out[0, lo, :] = self.added(1, lo).astype(BF16)
        self.over = [hops.start(out.at[0, lo], self.from_y.at[lo], y)]
        self.far[2].wait_recv()
        out[1, hi, :] = crossed(self.added(2, hi), group).astype(BF16)
        self.over.append(hops.start(out.at[1, hi], self.from_z.at[hi], z))

    def eight_middle(self):
        hops, out, group = self.hops, self.out, self.group
        lo, hi = self.halves()
        self.diag_y.wait_recv()
        out[1, lo, :] = crossed(self.added(2, lo) + self.part_y[...].astype(F32), group).astype(BF16)
        self.over.append(hops.start(out.at[1, lo], self.from_z.at[lo], hops.to(2)))
        self.diag_z.wait_recv()
        out[0, hi, :] = (self.added(1, hi) + self.part_z[...].astype(F32)).astype(BF16)
        self.over.append(hops.start(out.at[0, hi], self.from_y.at[hi], hops.across()))

    def eight_end(self):
        self.far[0].wait_recv()
        for copy in self.over:
            copy.wait_recv()
        total = (
            self.partial[0].astype(F32)
            + self.core[0].astype(F32)
            + self.from_y[...].astype(F32)
            + self.from_z[...].astype(F32)
        )
        self.hops.sent(list(self.far.values()) + [self.diag_y, self.diag_z] + self.over)
        return total


QKV, OUT, GU, DOWN = range(4)
IS_SHARED = (False, False, True, True)


def others(k, kinds):
    return [k] + (list(range(4, kinds)) if k == 1 else [])


class Gather:
    def __init__(self, hops, local, count, packs, crossed_over, full):
        self.hops, self.local, self.packs, self.over, self.full = hops, local, packs, crossed_over, full
        self.kinds = count // 2
        self.arrived, self.have = {}, set()
        self.half = lax.rem(hops.index["dp"] // 2, 2)
        self.rows = packs[0].shape[-2]

    def cross(self, a):
        hops = self.hops
        self.arrived[a] = hops.start(self.packs[a].at[hops.other], self.over[a], hops.across())

    def block(self, a, layer, r):
        return self.full[layer][a].at[pl.ds(r * self.rows, self.rows)]

    def source(self, a, other):
        if a not in self.have:
            self.have.add(a)
            self.arrived[a].wait_recv()
        section = self.hops.index["section"]
        if not IS_SHARED[a]:
            return self.packs[a].at[section], self.over[a]
        which = 1 - self.half if other else self.half
        return self.packs[a].at[section, which], self.over[a].at[which]

    def straight(self, a, layer):
        first, second = self.source(a, False)
        here = self.hops.index["section"] == layer
        self.arrived[a, layer, "x", 0] = self.hops.start_either(
            here, first, second, self.block(a, layer, 1), self.hops.to(1)
        )

    def begin(self, a, layer, step):
        for k in others(step, self.kinds):
            if IS_SHARED[a] or k == 1 or k % 2 == 0:
                first, second = self.source(a, k % 2 == 1)
                self.arrived[a, layer, k] = self.hops.start_either(
                    self.hops.index["section"] == layer,
                    first,
                    second,
                    self.block(a, layer, 2 * k),
                    self.hops.to(2 * k),
                )

    def onward(self, a, layer, step):
        hops = self.hops
        for k in others(step, self.kinds):
            self.arrived[a, layer, k].wait_recv()
            self.arrived[a, layer, "x", k] = hops.start(
                self.block(a, layer, 2 * k), self.block(a, layer, 2 * k + 1), hops.to(1)
            )
            if not IS_SHARED[a] and k % 2 == 0:
                self.arrived[a, layer, k + 1] = hops.start(
                    self.block(a, layer, 2 * k), self.block(a, layer, 2 * k + 2), hops.to(2)
                )

    def complete(self, a, layer):
        for k in range(self.kinds):
            self.arrived[a, layer, "x", k].wait_recv()

    def parts(self, a, layer, target):
        first, second = self.source(a, False)
        rest = pl.ds(self.rows, target.shape[0] - self.rows)
        here = self.hops.index["section"] == layer
        return [
            (here, first, second, target.at[pl.ds(0, self.rows)]),
            (self.full[layer][a].at[rest], target.at[rest]),
        ]


def attention_step(heads, qkv, place, cos, sin, visible, rotated, log_total):
    width = heads * HEAD_SIZE
    keys = rope(qkv[width : width + HEAD_SIZE, place], cos, sin).astype(BF16)
    values = qkv[width + HEAD_SIZE :, place].astype(BF16)
    rotated[width : width + HEAD_SIZE, place] = keys
    rotated[width + HEAD_SIZE :, place] = values
    attended = []
    for h in range(heads):
        at = slice(h * HEAD_SIZE, (h + 1) * HEAD_SIZE)
        queries = rope(qkv[at, place], cos, sin).astype(BF16)
        rotated[at, place] = queries
        score = dot_tn(keys, queries)
        score = jnp.where(visible, score * FACTOR, MASK_FILL)
        top = jnp.max(score, 0, keepdims=True)
        exponent = jnp.exp(score - top)
        total = jnp.sum(exponent, 0, keepdims=True)
        prob = (exponent * (1.0 / total)).astype(BF16)
        attended.append(dot_n(values, prob))
        log_total[h : h + 1, place] = top + jnp.log(total)
    return jnp.concatenate(attended, 0).T.astype(BF16)


def attention_back_step(heads, rotated, grad_att, place, cos, sin, visible, log_total):
    width = heads * HEAD_SIZE
    keys = rotated[width : width + HEAD_SIZE, place]
    values = rotated[width + HEAD_SIZE :, place]
    length = keys.shape[1]
    grad_keys = jnp.zeros((HEAD_SIZE, length), F32)
    grad_values = jnp.zeros((HEAD_SIZE, length), F32)
    found = []
    for h in range(heads):
        at = slice(h * HEAD_SIZE, (h + 1) * HEAD_SIZE)
        queries = rotated[at, place]
        grad = grad_att[at, :]
        score = jnp.where(visible, dot_tn(keys, queries) * FACTOR, MASK_FILL)
        prob = jnp.exp(score - log_total[h : h + 1, place])
        grad_prob = dot_tn(values, grad)
        inner = jnp.sum(prob * grad_prob, 0, keepdims=True)
        grad_score = (FACTOR * prob * (grad_prob - inner)).astype(BF16)
        found.append(rope_back(dot_n(keys, grad_score), cos, sin))
        grad_keys += dot_t(queries, grad_score)
        grad_values += dot_t(grad, prob.astype(BF16))
    found += [rope_back(grad_keys, cos, sin), grad_values]
    return jnp.concatenate(found, 0).T.astype(BF16)


def steps_of(names):
    found = []
    for name in names:
        letters = name.rstrip("0123456789")
        found.append((letters, *(int(digit) for digit in name[len(letters) :])))
    return found


ORDER = (
    "c0", "c1", "B002", "B001", "B012", "c2", "O001", "O002", "B102", "c3", "B112", "X20",
    "O003", "B101", "O102", "B302", "n0", "m0", "X00", "a0", "B201", "X30", "B301", "X01",
    "X10", "O112", "B203", "O103", "B303", "O101", "B202", "e0", "O201", "q0", "O302", "O203",
    "X11", "r0", "g0", "O303", "h0", "B111", "O202", "B011", "O301", "X21", "B213", "i0",
    "B312", "O011", "u0", "d0", "s0", "O111", "t0", "O012", "O113", "B211", "B311", "v0",
    "a1", "n1", "O013", "B212", "X31", "e1", "O213", "q1", "O211", "r1", "g1", "h1",
    "B313", "O212", "O311", "O312", "m1", "i1", "g2", "u1", "h2", "O313", "i2", "bl1",
    "S31", "E31", "bk1", "bp1", "bs1", "S21", "bt1", "Z313", "Z310", "Z311", "Z312", "bv1",
    "E21", "ba1", "Z211", "be1", "bq1", "Z212", "E11", "S01", "E01", "br1", "bg1", "bh1",
    "Z011", "Z213", "Y31", "S11", "Z013", "bi1", "bl0", "S30", "bk0", "Z210", "Z110", "Z113",
    "Y21", "E30", "Z111", "Z012", "bp0", "bs0", "Z302", "S20", "bt0", "E20", "Z300", "Z301",
    "Z112", "bv0", "ba0", "Z010", "Z303", "Z201", "Y11", "Y01", "be0", "Z202", "bq0", "S00",
    "S10", "br0", "bn0", "bn1", "Y30", "E10", "Z203", "E00", "Z003", "d1", "Z001", "Z200",
    "bn2", "s1", "Z002", "Z103", "Y20", "Z000", "Z101", "bn3", "Z100", "Z102", "Y00", "bn4",
    "t1", "Y10", "v1", "bn5", "w0", "w1",
)


def into_partial(block, w, partial, here, width, tile):
    @pl.loop(0, width // tile)
    def _(n):
        cut = pl.ds(pl.multiple_of(n * tile, tile), tile)
        some = dot_t(block[...], w[cut, :])
        partial[:, :, cut] = some.astype(BF16).reshape(partial.shape[0], here, tile)


def add_rows(target, left, right):
    rows = target.shape[0]
    step = min(32, rows)

    @pl.loop(0, rows // step)
    def _(i):
        at = pl.ds(pl.multiple_of(i * step, step), step)
        target[at, :] = (left[at, :].astype(F32) + right[at, :].astype(F32)).astype(BF16)


class Scatter:
    def __init__(self, hops, local, kept, staged, landed, distant, sums_out, one_block, term, rows):
        self.hops, self.local, self.kept, self.staged = hops, local, kept, staged
        self.landed, self.distant, self.sums_out = landed, distant, sums_out
        self.one_block, self.term, self.rows = one_block, term, rows
        self.kinds = kept[0].shape[0]
        self.half = lax.rem(hops.index["dp"] // 2, 2)
        self.section = hops.index["section"]
        self.copies, self.ending = {}, []

    def renew(self, a):
        assert (a, 1) in [entry[:2] for entry in self.ending]
        out = [self.copies[a, 1, "z", k] for k in range(1, self.kinds)]
        self.hops.sent([copy for copy in out if copy is not None])
        for b, layer, keep, away in self.ending:
            if (b, layer) == (a, 1):
                pl.when(self.section == layer)(keep.wait)
                pl.when(self.section != layer)(away.wait_send)

    def stage(self, a, layer):
        hops, local, rows, kept = self.hops, self.local, self.rows, self.kept
        if layer == 0 and rows % 128:
            self.renew(a)
        base, at = hops.claim(self.kinds), local.claim(self.kinds)
        cols = pl.ds(0, kept[a].shape[-1])
        source, target = self.staged[layer][a], self.landed[layer][a]

        @pl.loop(0, self.kinds)
        def _(k):
            if rows % 128:
                both = self.term(a, 2 * k, 2 * rows)
                self.one_block[:, cols] = both[rows:]
                kept[a][k] = both[:rows]
            else:
                self.one_block[:, cols] = self.term(a, 2 * k + 1, rows)
            keep = pltpu.make_async_copy(
                self.one_block.at[:, cols], source.at[k], local.sems.at[at + k]
            )
            keep.start()
            keep.wait()
            hops.at(source.at[k], target.at[k], hops.to(1), base + k).start()

        for k in range(self.kinds):
            copy = hops.at(source.at[k], target.at[k], hops.to(1), base + k)
            self.copies[a, layer, "x", k] = copy
            hops.started.append(copy)

    def evens(self, a, layer):
        if self.rows % 128:
            return
        if layer == 0:
            self.renew(a)

        @pl.loop(0, self.kinds)
        def _(k):
            self.kept[a][k] = self.term(a, 2 * k, self.rows)

    def fetch(self, a, source):
        block = self.one_block.at[:, pl.ds(0, self.kept[a].shape[-1])]
        self.local.now((source, block))
        return block

    def meet(self, a, layer, step):
        hops, kept, copies = self.hops, self.kept[a], self.copies
        far = self.distant[layer][a]
        steps = [0] if step == 0 else list(reversed(others(step, self.kinds)))
        for k in steps:
            copies[a, layer, "x", k].wait_recv()
            add_rows(kept.at[k], kept.at[k], self.fetch(a, self.landed[layer][a].at[k]))
            if not IS_SHARED[a] and k % 2 == 0 and k:
                copies[a, layer, "z", k + 1].wait_recv()
                add_rows(kept.at[k], kept.at[k], self.fetch(a, far.at[k + 1]))
            if k:
                passed = not IS_SHARED[a] and k % 2 == 1 and k > 1
                copies[a, layer, "z", k] = hops.start(
                    kept.at[k], far.at[k], hops.to(2 if passed else 2 * k)
                )

    def deliver(self, a, layer):
        hops, kept, copies = self.hops, self.kept[a], self.copies
        far = self.distant[layer][a]
        mine, other = [], []
        for k in range(1, self.kinds):
            if IS_SHARED[a] or k == 1 or k % 2 == 0:
                copies[a, layer, "z", k].wait_recv()
                (other if IS_SHARED[a] and k % 2 else mine).append(k)
        for k in mine:
            add_rows(kept.at[0], kept.at[0], self.fetch(a, far.at[k]))
        pieces = [kept.at[0]]
        if IS_SHARED[a]:
            hops.sent([copies[a, layer, "z", 1]])
            copies[a, layer, "z", 1] = None
            self.local.now((far.at[other[0]], kept.at[1]))
            for k in other[1:]:
                add_rows(kept.at[1], kept.at[1], self.fetch(a, far.at[k]))
            pieces.append(kept.at[1])
        for number, piece in enumerate(pieces):
            which = self.half if number == 0 else 1 - self.half
            target = self.sums_out[a].at[self.section]
            if IS_SHARED[a]:
                target = self.sums_out[a].at[self.section, which]
            keep = self.local.make(piece, target)
            away = hops.at(piece, target, hops.across(), hops.claim())
            pl.when(self.section == layer)(keep.start)
            pl.when(self.section != layer)(away.start)
            self.ending.append((a, layer, keep, away))

    def end(self):
        for a, layer, keep, away in self.ending:
            pl.when(self.section == layer)(away.wait_recv)
            if layer == 0:
                pl.when(self.section == layer)(keep.wait)
                pl.when(self.section != layer)(away.wait_send)


def layers_kernel(count, heads, group, *refs):
    refs = list(refs)
    take = lambda number: [refs.pop(0) for _ in range(number)]
    packs, raw_rows, raw_gains = take(4), take(2), take(2)
    cosine, sine, owner_col, owner_row = take(4)
    ends, sums_out = take(2), take(4)
    crossed_over, full = take(4), (take(4), take(4))
    rows_attn_out, hidden_out, (rows_mlp_out, gate_up_out, grad_out) = take(2), take(2), take(3)
    staged, landed, distant = [(take(4), take(4)) for _ in range(3)]
    gain_sums = take(2)
    send, recv, sems = take(3)
    w_low, w_out, w_gu = take(3)
    slots4, slots8, partial, rows_mlp = take(4)
    qkv, gate_up, hidden = take(3)
    rotated, attended, log_total, middles = [take(2) for _ in range(4)]
    grad_att, grad_qkv = take(2)
    kept, (one_block,) = take(4), take(1)
    entering, handed, grad_middle = take(3)
    raw_whole, cotangent, through = take(3)
    gain_whole, gains, gain_terms, gain_landed = take(4)
    own, turned, core, out, from_y, from_z, part_y, part_z, last_z, last_part = take(10)
    hops, local = Hops(send, recv), Local(sems)
    hops.greet(reached(count))
    spread = Spread(hops, local, own, turned, group)
    sums = Sums(hops, partial, core, out, from_y, from_z, part_y, part_z, group)
    sums_last = Sums(hops, partial, core, out, from_y, last_z, part_y, last_part, group)
    gather = Gather(hops, local, count, packs, crossed_over, full)
    section = hops.index["section"]
    here, width = own.shape
    rows = width // count
    length = cosine.shape[1]
    seqs = slots4.shape[0] * here // length
    per_seq = length // here
    tile = 512
    units = hidden.shape[1]
    real = gate_up.shape[1] // 2
    whole = real // 128
    rest = real - whole * 128
    split = rotated[0].shape[0]
    rows_attn = partial.at[pl.ds(4, 4)]
    stores = []

    def store(source, target):
        stores.append(local.start(source, target))

    def settle():
        for copy in stores:
            copy.wait()
        stores.clear()

    def span(i, size):
        return pl.ds(pl.multiple_of(i * size, size), size)

    w_qkv = w_low.at[:, pl.ds(0, split)]

    def project(layer):
        gather.complete(QKV, layer)
        gather.complete(OUT, layer)
        local.now(*gather.parts(QKV, layer, w_qkv), *gather.parts(OUT, layer, w_out))

        @pl.loop(0, seqs)
        def _(i):
            block = slots4[pl.ds(i * per_seq, per_seq)].reshape(length, width)
            place = span(i, length)
            qkv[:, place] = dot_n(block, w_low[:, :split]).T
            visible = visible_block(owner_col[i], owner_row[i])
            attended[layer][place, :] = attention_step(
                heads, qkv, place, cosine[...], sine[...], visible, rotated[layer], log_total[layer]
            )

        store(slots4, rows_attn_out[layer])

        @pl.loop(0, width // tile)
        def _(n):
            cut = span(n, tile)
            for i in range(seqs):
                some = dot_t(attended[layer][i * length : (i + 1) * length, :], w_out[cut, :])
                partial[i * per_seq : (i + 1) * per_seq, :, cut] = some.astype(BF16).reshape(
                    per_seq, here, tile
                )

    def expand(layer):
        gather.complete(GU, layer)
        local.now(*gather.parts(GU, layer, w_gu))

        block = slots8[...].reshape(slots8.shape[0] * here, width)

        @pl.loop(0, whole)
        def _(n):
            cut = span(n, 256)
            both = dot_n(block, w_gu[:, cut])
            gate_up[:, cut] = both.astype(BF16)
            gate, up = both[:, :128], both[:, 128:]
            hidden[:, span(n, 128)] = (gate * jax.nn.sigmoid(gate) * up).astype(BF16)

        if rest:
            both = dot_n(block, w_gu[:, whole * 256 :])
            gate_up[:, whole * 256 :] = both.astype(BF16)
            gate, up = both[:, :rest], both[:, rest:]
            some = (gate * jax.nn.sigmoid(gate) * up).astype(BF16)
            hidden[:, whole * 128 :] = jnp.concatenate([some, jnp.zeros_like(some)], 1)

        if layer == 0:
            store(slots8, rows_mlp_out)
            store(gate_up, gate_up_out)
        else:
            rows_mlp[...] = slots8[...]
        store(hidden, hidden_out[layer])

    def entry(layer):
        return entering if layer == 0 else handed

    waiting = {}

    def bring(number):
        target = raw_whole.at[:, span(section, width // 2)]
        waiting[number] = [
            hops.start(raw_rows[number].at[hops.other, 0], target, hops.across()),
            local.start(raw_rows[number].at[section, 0], target),
        ]
        if number == 0:
            for kind in range(2):
                waiting[number] += [
                    hops.start(raw_gains[kind], gain_whole.at[section, kind], hops.across()),
                    local.start(raw_gains[kind], gain_whole.at[section, kind]),
                ]

    def brought(number):
        for place, copy in enumerate(waiting[number]):
            copy.wait() if place % 2 else copy.wait_recv()
        rows_here = reordered(raw_whole[...].astype(F32), count)
        if number == 0:
            entering[...] = rows_here
            for layer in range(2):
                for kind in range(2):
                    mark = 2 * layer + kind
                    gains[mark : mark + 1, :] = reordered(gain_whole[layer, kind], count)
        else:
            cotangent[...] = rows_here.astype(BF16)

    def gain(layer, kind):
        mark = 2 * layer + kind
        return gains[mark : mark + 1, :]

    def ready(layer):
        settle()
        if layer == 1:
            local.now((grad_out, slots8))
        else:
            local.now((gate_up_out, gate_up), (hidden_out[0], hidden), (rows_mlp_out, rows_mlp))

    def widen(layer):
        if layer == 1:
            gather.complete(DOWN, 1)
        local.now(*gather.parts(DOWN, layer, w_low))

        @pl.loop(0, slots8.shape[0] // 2)
        def _(c):
            block = slots8[pl.ds(c * 2, 2)].reshape(2 * here, width)
            place = span(c, 2 * here)
            grad_hidden = dot_n(block, w_low[...]).astype(BF16).astype(F32)

            def back(grad, gate, up):
                gate, up = gate.astype(F32), up.astype(F32)
                sig = jax.nn.sigmoid(gate)
                return [
                    (grad * up * sig * (1.0 + gate * (1.0 - sig))).astype(BF16),
                    (grad * (gate * sig)).astype(BF16),
                ]

            for n in range(whole):
                at = slice(n * 256, n * 256 + 256)
                both = gate_up[place, at]
                gate_up[place, at] = jnp.concatenate(
                    back(grad_hidden[:, n * 128 : n * 128 + 128], both[:, :128], both[:, 128:]), 1
                )
            if rest:
                both = gate_up[place, whole * 256 :]
                gate_up[place, whole * 256 :] = jnp.concatenate(
                    back(grad_hidden[:, whole * 128 : real], both[:, :rest], both[:, rest:]), 1
                )

    def attend(layer):
        local.now(
            *gather.parts(OUT, layer, w_out),
            *gather.parts(QKV, layer, w_qkv),
            (rows_attn_out[layer], rows_attn),
        )

        @pl.loop(0, seqs)
        def _(i):
            block = slots4[pl.ds(i * per_seq, per_seq)].reshape(length, width)
            place = span(i, length)
            grad_att[...] = dot_n(block, w_out[...]).T.astype(BF16)
            visible = visible_block(owner_col[i], owner_row[i])
            grad_qkv[place, :] = attention_back_step(
                heads, rotated[layer], grad_att, place, cosine[...], sine[...], visible, log_total[layer]
            )

        @pl.loop(0, width // tile)
        def _(n):
            cut = span(n, tile)
            for i in range(seqs):
                some = dot_t(grad_qkv[i * length : (i + 1) * length, :], w_low[cut, :split])
                partial[i * per_seq : (i + 1) * per_seq, :, cut] = some.astype(BF16).reshape(
                    per_seq, here, tile
                )

    working = [1]

    def term(a, r, size):
        slots, right = {
            QKV: (rows_attn, grad_qkv),
            OUT: (slots4, attended[working[0]]),
            GU: (rows_mlp, gate_up),
            DOWN: (slots8, hidden),
        }[a]
        cut = pl.ds(pl.multiple_of(r * rows, max(rows, 128)), size)
        return dot_tn(slots[:, :, cut].reshape(slots.shape[0] * here, size), right[...]).astype(BF16)

    scatter = Scatter(
        hops, local, kept, staged, landed, distant, sums_out, one_block, term, rows
    )

    def back_through(total, source, values, layer, kind, result):
        into, term_row = norm_back(total, values, gain(layer, kind))
        mark = 2 * layer + kind
        gain_terms[0, mark : mark + 1, :] = term_row
        result[...] = (source + into).astype(result.dtype)

    leaving = []

    def leave(number, block):
        block[...] = reordered(block[...].astype(F32), count).astype(BF16)
        target = ends[number].at[section, 0]
        leaving.append(local.start(block.at[:, span(section, width // 2)], target))
        leaving.append(hops.start(block.at[:, span(hops.other, width // 2)], target, hops.across()))

    gain_places, offset = [hops.core(), hops.across()], 1
    while offset < count:
        gain_places.append(hops.to(offset))
        offset *= 2
    gain_moves = []

    def add_gains(step):
        for number in range(step, len(gain_places) + 1) if step == 5 else [step]:
            if number == 0:
                gain_terms[0] = reordered(gain_terms[0], count)
            else:
                gain_moves[-1].wait_recv()
                gain_terms[number] = gain_terms[number - 1] + gain_landed[number - 1]
            if number < len(gain_places):
                gain_moves.append(
                    hops.start(gain_terms.at[number], gain_landed.at[number], gain_places[number])
                )
        if step == 5:
            total = gain_terms[len(gain_places)]
            mine = jnp.where(section == 0, total[0:2], total[2:4])
            for kind in range(2):
                gain_sums[kind][...] = mine[kind : kind + 1]

    for name, *at in steps_of(ORDER):
        layer = at[0]
        if name == "c":
            gather.cross(*at)
        elif name == "X":
            gather.straight(*at)
        elif name == "B":
            gather.begin(*at)
        elif name == "O":
            gather.onward(*at)
        elif name == "n":
            bring(*at)
        elif name == "m":
            brought(*at)
        elif name == "a":
            spread.four(normed(entry(layer)[...], gain(layer, 0)), slots4)
        elif name in ("e", "be"):
            spread.four_end(slots4)
        elif name == "q":
            project(layer)
        elif name == "r":
            middles[layer][...] = entry(layer)[...] + sums.four()
        elif name == "g":
            if layer == 2:
                spread.eight(cotangent[...], grad_out)
            else:
                spread.eight(normed(middles[layer][...], gain(layer, 1)), slots8)
        elif name == "h":
            spread.eight_middle(grad_out if layer == 2 else slots8)
        elif name == "i":
            spread.eight_end(grad_out if layer == 2 else slots8)
        elif name == "u":
            expand(layer)
        elif name == "d":
            if layer == 0:
                gather.complete(DOWN, 0)
            else:
                local.now((hidden_out[1], hidden))
            local.now(*gather.parts(DOWN, layer, w_low))
            into_partial(hidden, w_low, partial, here, width, tile // 2)
        elif name == "s":
            settle()
            (sums_last if layer == 1 else sums).eight()
        elif name == "t":
            (sums_last if layer == 1 else sums).eight_middle()
        elif name == "v":
            if layer == 1:
                raw_whole[...] = (middles[1][...] + sums_last.eight_end()).astype(BF16)
            else:
                handed[...] = (middles[0][...] + sums.eight_end()).astype(BF16).astype(F32)
        elif name == "bl":
            working[0] = layer
            ready(layer)
        elif name == "bk":
            widen(layer)
        elif name == "S":
            scatter.stage(*at)
        elif name == "E":
            scatter.evens(*at)
        elif name == "Z":
            scatter.meet(*at)
        elif name == "Y":
            scatter.deliver(*at)
        elif name == "bp":
            if layer == 0:
                local.now(*gather.parts(GU, 0, w_gu))
            into_partial(gate_up, w_gu, partial, here, width, tile // 2)
        elif name == "bs":
            sums.eight()
        elif name == "bt":
            sums.eight_middle()
        elif name == "bv":
            total = sums.eight_end()
            source = (cotangent if layer == 1 else through)[...].astype(F32)
            back_through(total, source, middles[layer][...], layer, 1, grad_middle)
        elif name == "ba":
            spread.four(grad_middle[...].astype(BF16), slots4)
        elif name == "bq":
            attend(layer)
        elif name == "br":
            back_through(sums.four(), grad_middle[...], entry(layer)[...], layer, 0, through)
        elif name == "bg":
            spread.eight(through[...], slots8)
        elif name == "bh":
            spread.eight_middle(slots8)
        elif name == "bi":
            spread.eight_end(slots8)
        elif name == "w":
            leave(layer, (raw_whole, through)[layer])
        elif name == "bn":
            add_gains(layer)
    scatter.end()
    settle()
    for place, copy in enumerate(leaving):
        copy.wait_recv() if place % 2 else copy.wait()
    hops.drain()


def both_layers(packs, raw, tables, owners):
    count = lax.axis_size("dp")
    kinds = count // 2
    anywhere = pl.BlockSpec(memory_space=pl.ANY)
    inside = pl.BlockSpec(memory_space=pltpu.VMEM)
    seqs, length = owners.shape
    tokens = seqs * length
    here, width = tokens // 4, packs[0].shape[-2] * count
    rows = width // count
    columns = [pack.shape[-1] for pack in packs]
    head_width = columns[OUT]
    heads = head_width // HEAD_SIZE
    group = 2 * width // count
    shape = lambda *dims: jax.ShapeDtypeStruct(dims, BF16)
    ends = [shape(*raw[0].shape)] * 2
    sums = [shape(*((2, 2) if IS_SHARED[a] else (2,)), rows, columns[a]) for a in range(4)]
    full = [shape(width, columns[a]) for a in range(4)] * 2
    rest = (
        [shape(4, here, width)] * 2
        + [shape(8 * here, columns[DOWN])] * 2
        + [shape(8, here, width), shape(8 * here, columns[GU]), shape(8, here, width)]
    )
    blocks = [shape(kinds, rows, columns[a]) for a in range(4)] * 6
    far = ends + sums + [shape(*pack.shape[1:]) for pack in packs] + full + rest + blocks
    near = [jax.ShapeDtypeStruct((1, width), F32)] * 2
    inner = lambda *dims: pltpu.VMEM(dims, BF16)
    block = lambda *lead: pltpu.VMEM(lead + (here, width), BF16)
    wide = pltpu.VMEM((here, width), F32)
    wires = 2 * 8 * count + 8 * kinds + 6 * (12 + width // group) + 80
    scratch = [
        pltpu.SemaphoreType.DMA((wires,)),
        pltpu.SemaphoreType.DMA((wires,)),
        pltpu.SemaphoreType.DMA((8 * kinds + 60,)),
        inner(width, columns[DOWN]),
        inner(width, columns[OUT]),
        inner(width, columns[GU]),
        block(4),
        block(8),
        block(8),
        block(8),
        pltpu.VMEM((columns[QKV], tokens), F32),
        inner(8 * here, columns[GU]),
        inner(8 * here, columns[DOWN]),
    ]
    scratch += [inner(columns[QKV], tokens)] * 2 + [inner(tokens, head_width)] * 2
    scratch += [pltpu.VMEM((heads, tokens), F32)] * 2 + [wide] * 2
    scratch += [inner(head_width, length), inner(tokens, columns[QKV])]
    scratch += [inner(kinds, rows, columns[a]) for a in range(4)] + [inner(rows, max(columns))]
    scratch += [wide] * 3 + [block()] * 3
    sums_of = count.bit_length() + 1
    scratch += [
        pltpu.VMEM((2, 2, 1, width), F32),
        pltpu.VMEM((4, width), F32),
        pltpu.VMEM((sums_of + 1, 4, width), F32),
        pltpu.VMEM((sums_of, 4, width), F32),
    ]
    part = inner(here // 2, width)
    scratch += [block(), block(), block(4), block(3), block(), block(), part, part, block(), part]
    results = pl.pallas_call(
        functools.partial(layers_kernel, count, heads, group),
        out_shape=far + near,
        in_specs=[anywhere] * 8 + [inside] * 4,
        out_specs=[anywhere] * len(far) + [inside] * 2,
        scratch_shapes=scratch,
        compiler_params=pltpu.CompilerParams(
            collective_id=0, has_side_effects=True, vmem_limit_bytes=62 * 1024 * 1024
        ),
    )(*packs, *raw, *tables, owners[:, :, None], owners[:, None, :])
    return results[:2], results[2:6], results[-2:]


def unit_tiles(units, section, shared):
    tiles = units // 256
    first = section * units // 128 + shared * tiles
    return [(first + j) * 128 for j in range(tiles)], section * units + 256 * tiles + shared * 64


def pack_kernel(w_query, keyval, w_out, w_gate_up, w_down, qkv, out, gate_up, down):
    half = qkv.shape[2] - 2 * HEAD_SIZE
    units = w_down.shape[2] // 2
    for section in range(2):
        at = slice(section * half, (section + 1) * half)
        place = slice(section * HEAD_SIZE, (section + 1) * HEAD_SIZE)
        qkv[section, :, :half] = w_query[0, :, at]
        qkv[section, :, half:] = jnp.concatenate([keyval[0, :, 0, place], keyval[0, :, 1, place]], 1)
        out[section] = w_out[0, :, at]
        for shared in range(2):
            tiles, tail = unit_tiles(units, section, shared)
            for j, first in enumerate(tiles):
                for kind in range(2):
                    at = slice(256 * j + 128 * kind, 256 * j + 128 * kind + 128)
                    gate_up[section, shared, :, at] = w_gate_up[0, :, kind, first : first + 128]
                down[section, shared, :, 128 * j : 128 * j + 128] = w_down[0, :, first : first + 128]
            end = slice(tail, tail + 64)
            gate_up[section, shared, :, 256 * len(tiles) :] = jnp.concatenate(
                [w_gate_up[0, :, 0, end], w_gate_up[0, :, 1, end]], 1
            )
            some = w_down[0, :, end]
            down[section, shared, :, 128 * len(tiles) :] = jnp.concatenate(
                [some, jnp.zeros_like(some)], 1
            )


def unpack_kernel(qkv, out, gate_up, down, w_query, keyval, w_out, w_gate_up, w_down):
    half = qkv.shape[2] - 2 * HEAD_SIZE
    units = w_down.shape[2] // 2
    for section in range(2):
        at = slice(section * half, (section + 1) * half)
        w_query[0, :, at] = qkv[section, :, :half].astype(F32)
        w_out[0, :, at] = out[section].astype(F32)
        for shared in range(2):
            tiles, tail = unit_tiles(units, section, shared)
            for j, first in enumerate(tiles):
                for kind in range(2):
                    at = slice(256 * j + 128 * kind, 256 * j + 128 * kind + 128)
                    w_gate_up[0, :, kind, first : first + 128] = gate_up[section, shared, :, at].astype(F32)
                w_down[0, :, first : first + 128] = down[section, shared, :, 128 * j : 128 * j + 128].astype(F32)
        tiles, tail = unit_tiles(units, section, 0)
        last = slice(256 * len(tiles), 256 * len(tiles) + 128)
        both = [gate_up[section, shared, :, last].astype(F32) for shared in range(2)]
        w_gate_up[0, :, 0, tail : tail + 128] = jnp.concatenate([both[0][:, :64], both[1][:, :64]], 1)
        w_gate_up[0, :, 1, tail : tail + 128] = jnp.concatenate([both[0][:, 64:], both[1][:, 64:]], 1)
        at = slice(128 * len(tiles), 128 * len(tiles) + 64)
        w_down[0, :, tail : tail + 128] = jnp.concatenate(
            [down[section, shared, :, at].astype(F32) for shared in range(2)], 1
        )
    for kind in range(2):
        start = half + kind * HEAD_SIZE
        keyval[0, :, kind, :] = jnp.concatenate(
            [qkv[section, :, start : start + HEAD_SIZE].astype(F32) for section in range(2)], 1
        )


def row_specs(shapes, step):
    specs = []
    for dims, axis in shapes:
        block = tuple(step if i == axis else size for i, size in enumerate(dims))
        specs.append(
            pl.BlockSpec(block, functools.partial(lambda n, a, i: tuple(i if k == a else 0 for k in range(n)), len(dims), axis))
        )
    return specs


def packed(raw, kernel, outs, raw_first):
    rows = raw[0].shape[1] if raw_first else raw[0].shape[-2]
    step = min(rows, 64)
    wide = [(block.shape, 1) for block in (raw if raw_first else outs)]
    narrow = [(block.shape, len(block.shape) - 2) for block in (outs if raw_first else raw)]
    first, second = row_specs(wide, step), row_specs(narrow, step)
    return pl.pallas_call(
        kernel,
        grid=(rows // step,),
        out_shape=outs,
        in_specs=first if raw_first else second,
        out_specs=second if raw_first else first,
        compiler_params=pltpu.CompilerParams(vmem_limit_bytes=40 * 1024 * 1024),
    )(*raw)


def shards(
    layer_in,
    out_grad,
    doc_lengths,
    attn_gain,
    w_query,
    keyval_weight,
    w_out,
    mlp_gain,
    w_gate_up,
    w_down,
):
    micro, seqs, here, columns = layer_in.shape
    length = here * lax.axis_size("tensor")
    rows = w_query.shape[1]
    head_width = w_query.shape[2] // 2
    units = w_down.shape[2] // 4
    shape = jax.ShapeDtypeStruct
    raw = [w_query, keyval_weight, w_out, w_gate_up, w_down]
    packs = packed(
        raw,
        pack_kernel,
        [
            shape((2, rows, head_width + 2 * HEAD_SIZE), BF16),
            shape((2, rows, head_width), BF16),
            shape((2, 2, rows, 2 * units), BF16),
            shape((2, 2, rows, units + -units % 128), BF16),
        ],
        True,
    )
    owners = owners_of(doc_lengths.reshape(micro * seqs, -1), length)
    tables = rope_tables(length)
    (layer_out, in_grad), sums, (attn_term, mlp_term) = both_layers(
        packs, [layer_in, out_grad, attn_gain, mlp_gain], tables, owners
    )
    grads = packed(sums, unpack_kernel, [shape(block.shape, F32) for block in raw], False)
    grad_q, grad_kv, grad_o, grad_gu, grad_d = grads
    return layer_out, in_grad, attn_term, grad_q, grad_kv, grad_o, mlp_term, grad_gu, grad_d


def solution(mesh):
    activation = P(None, "dp", "tensor", "section")
    matrix = P("section", "dp", "tensor")
    stacked = P("section", "dp", None, "tensor")
    gain = P("section", None)
    return jax.shard_map(
        shards,
        mesh=mesh,
        in_specs=(
            activation,
            activation,
            P(None, "dp", None),
            gain,
            matrix,
            stacked,
            matrix,
            gain,
            stacked,
            matrix,
        ),
        out_specs=(
            activation,
            activation,
            gain,
            matrix,
            stacked,
            matrix,
            gain,
            stacked,
            matrix,
        ),
        check_vma=False,
    )
```

time: 3720 us -> 792 us (0.21)
  waiting for transfers between devices: 3070 us -> 0 us
  Pallas kernels: 0 us -> 757 us
  matrix products: 369 us -> 0 us
  other arithmetic: 111 us -> 1.81 us
  blocking collectives: 64.6 us -> 0 us
  local copies, waits for them, and re-layouts: 63.3 us -> 20.1 us
    reduce_scatter x24 -> x0, waiting for transfers between devices: 2170 us -> none  [the longest x12 2110 us: weight_term(): lax.psum_scatter(lax.dot_general(left_rows, right_rows, (((0,), (0,)), ((...]
    all_gather x17 -> x0, waiting for transfers between devices: 832 us -> none  [the longest x1 444 us: layer_forward(): lax.all_gather(w_gate_up, 'dp', axis=0, tiled=True)]
    pallas_call x0 -> x3, Pallas kernels: none -> 757 us  [the longest x1 741 us: both_layers(): pl.pallas_call(functools.partial(layers_kernel, count, heads, group), out...]
    dot_general x60 -> x0, matrix products: 364 us -> none  [the longest x12 88.8 us: weight_term(): lax.dot_general(left_rows, right_rows, (((0,), (0,)), ((), ())), preferre...]
    psum x1 -> x0, blocking collectives: 64.6 us -> none  [shards(): gain_summed = lax.psum((gain_totals[0], gain_totals[1]), ('dp', 'tensor'))]
    ppermute x6 -> x0, waiting for transfers between devices: 60.6 us -> none  [the longest x4 48.7 us: passed_along(): return lax.ppermute(block, axis, route)]
    convert_element_type x29 -> x0, other arithmetic: 37.4 us -> none  [the longest x3 7.88 us: layer_forward(): hidden = (jax.nn.silu(gate_up[:, 0]) * gate_up[:, 1]).astype(jnp.bfloat16)]
  transfers between devices with their start and end apart: 47 -> 0, of which waited for: 36 -> 0; matrix products, arithmetic and copies ran while one was open for 8% -> 0% of each run, Pallas kernels for 0% -> 0%
where the time goes in v2:
time: 792 us; the launch traced here: 779 us
  Pallas kernels  757 us (96%)
  local copies, waits for them, and re-layouts  20.1 us (3%)
    pallas_call x1, Pallas kernels, both_layers(): pl.pallas_call(functools.partial(layers_kernel, count, heads, group), out...  741 us
    unnamed x38, local copies, waits for them, and re-layouts  18.6 us

profile of v2, /device:TPU:0, one launch (start us, length us, event | category | flops | bytes accessed | tf_op | source)
XLA Modules:
  0.0 779.5 jit_solution(17933524529570545409)
XLA Ops:
  0.7 0.9 reduce_window_sum.14
  1.6 0.6 broadcast_in_dim.5.refs_11_
  2.4 0.7 pad_maximum_fusion
  3.0 0.9 copy.20.refs_10_
  3.9 1.8 copy-done.2
  5.7 1.4 copy-done.5
  7.1 1.0 copy-done.8
  8.1 1.0 copy-done.9
  9.2 0.9 copy-done.12
  10.1 9.2 %shard_map.169 = (bf16[2,256,640]{2,1,0:T(8,128)(2,1)S(1)}, bf16[2,256,512]{2,1,0:T(8,128)(2,1)S(1)}, bf16[2,2,256,1408]{3,2,1,0:T(8,128)(2,1)S(1)}, bf16[2,2,256,768]{3,2,1,0:T(8,128)(2,1)S(1)}) custom-call(bf16[1,256,1024]{2,1,0:T(8,128)(2,1)S(1)} %copy-done.8, bf16[1,256,2,128]{3,2,1,0:T(2,128)(2,1)S(1)} %copy-done.12, ...), custom_call_target="tpu_custom_call" | custom-call | tf_op jit(solution)/shard_map/pallas_call | solution.py:1139
  19.3 1.6 copy-done.1
  20.9 1.1 copy-done.4
  22.0 0.8 copy-done.7
  22.9 0.8 copy-done.11
  23.7 741.4 %shard_map.170 = (bf16[2,1,128,1024]{3,2,1,0:T(8,128)(2,1)}, bf16[2,1,128,1024]{3,2,1,0:T(8,128)(2,1)}, bf16[2,256,640]{2,1,0:T(8,128)(2,1)}, bf16[2,256,512]{2,...) custom-call(bf16[2,256,640]{2,1,0:T(8,128)(2,1)} %copy-done.7, ...), custom_call_target="tpu_custom_call" | custom-call | tf_op jit(solution)/shard_map/pallas_call | solution.py:1048
  765.1 1.8 copy-done
  766.9 1.4 copy-done.3
  768.3 1.1 copy-done.6
  769.4 1.0 copy-done.10
  770.4 6.1 shard_map.171
  776.5 0.8 copy.25
  777.3 0.8 copy.26
  778.1 0.6 copy.27
  778.7 0.6 copy.28
  (24 shorter events, 0.3 us)
Async XLA Ops:
  3.9 1.8 copy-start.2
  5.7 1.4 copy-start.5
  7.1 1.0 copy-start.8
  8.1 1.0 copy-start.9
  9.2 0.9 copy-start.12
  19.3 1.6 copy-start.1
  20.9 1.1 copy-start.4
  22.0 0.8 copy-start.7
  22.9 0.8 copy-start.11
  765.1 1.8 copy-start
  766.9 1.4 copy-start.3
  768.3 1.1 copy-start.6
  769.4 1.0 copy-start.10
  770.4 6.1 copy-start.14
  770.4 6.9 copy-start.13
  776.5 1.6 copy-start.16
  776.5 2.2 copy-start.15

commit v3 on v2

--- a/solution.py
+++ b/solution.py
@@ -477,21 +477,21 @@
 
 
 ORDER = (
-    "c0", "c1", "B002", "B001", "B012", "c2", "O001", "O002", "B102", "c3", "B112", "X20",
-    "O003", "B101", "O102", "B302", "n0", "m0", "X00", "a0", "B201", "X30", "B301", "X01",
-    "X10", "O112", "B203", "O103", "B303", "O101", "B202", "e0", "O201", "q0", "O302", "O203",
-    "X11", "r0", "g0", "O303", "h0", "B111", "O202", "B011", "O301", "X21", "B213", "i0",
-    "B312", "O011", "u0", "d0", "s0", "O111", "t0", "O012", "O113", "B211", "B311", "v0",
-    "a1", "n1", "O013", "B212", "X31", "e1", "O213", "q1", "O211", "r1", "g1", "h1",
-    "B313", "O212", "O311", "O312", "m1", "i1", "g2", "u1", "h2", "O313", "i2", "bl1",
-    "S31", "E31", "bk1", "bp1", "bs1", "S21", "bt1", "Z313", "Z310", "Z311", "Z312", "bv1",
-    "E21", "ba1", "Z211", "be1", "bq1", "Z212", "E11", "S01", "E01", "br1", "bg1", "bh1",
-    "Z011", "Z213", "Y31", "S11", "Z013", "bi1", "bl0", "S30", "bk0", "Z210", "Z110", "Z113",
-    "Y21", "E30", "Z111", "Z012", "bp0", "bs0", "Z302", "S20", "bt0", "E20", "Z300", "Z301",
-    "Z112", "bv0", "ba0", "Z010", "Z303", "Z201", "Y11", "Y01", "be0", "Z202", "bq0", "S00",
-    "S10", "br0", "bn0", "bn1", "Y30", "E10", "Z203", "E00", "Z003", "d1", "Z001", "Z200",
-    "bn2", "s1", "Z002", "Z103", "Y20", "Z000", "Z101", "bn3", "Z100", "Z102", "Y00", "bn4",
-    "t1", "Y10", "v1", "bn5", "w0", "w1",
+    "c0", "B002", "B001", "c1", "B012", "X01", "B102", "c2", "n0", "X00", "O001", "B101",
+    "O002", "X20", "B202", "O003", "B201", "m0", "X11", "B111", "c3", "O202", "O102", "B301",
+    "B011", "B303", "B203", "B312", "a0", "O101", "O103", "X10", "O201", "B112", "e0", "q0",
+    "O303", "O011", "r0", "O301", "X30", "g0", "n1", "h0", "O203", "B302", "m1", "O012",
+    "i0", "O112", "O302", "B212", "u0", "d0", "O113", "s0", "O111", "t0", "B211", "B311",
+    "B213", "O013", "O212", "v0", "B313", "a1", "X31", "e1", "O211", "X21", "q1", "r1",
+    "O213", "g1", "h1", "O311", "i1", "O313", "g2", "O312", "u1", "h2", "i2", "bl1",
+    "S31", "bk1", "bp1", "E31", "bs1", "S21", "bt1", "E21", "Z311", "bv1", "ba1", "Z313",
+    "be1", "bq1", "Z211", "Z312", "br1", "S11", "bg1", "bh1", "Z210", "Z213", "E11", "Z212",
+    "E01", "Z310", "Y31", "S01", "bi1", "bl0", "bk0", "S30", "E30", "bp0", "bs0", "Z113",
+    "Y21", "Z302", "Z013", "bt0", "Z111", "S20", "Z110", "Z011", "E20", "Z200", "Z303", "Z012",
+    "bv0", "ba0", "Z112", "be0", "Z010", "Z201", "Z301", "Y01", "Z203", "Y11", "bq0", "Z202",
+    "Z300", "E00", "S00", "E10", "br0", "bn0", "Y30", "bn1", "d1", "Z003", "bn2", "s1",
+    "S10", "Z000", "Y20", "Z002", "Z103", "Z001", "Z101", "Z102", "Z100", "t1", "Y00", "Y10",
+    "bn3", "w1", "bn4", "v1", "bn5", "w0",
 )
 
 
@@ -1142,7 +1142,7 @@
         out_shape=outs,
         in_specs=first if raw_first else second,
         out_specs=second if raw_first else first,
-        compiler_params=pltpu.CompilerParams(vmem_limit_bytes=40 * 1024 * 1024),
+        compiler_params=pltpu.CompilerParams(vmem_limit_bytes=62 * 1024 * 1024),
     )(*raw)
 
 

time: 792 us -> 763 us (0.963)
  local copies, waits for them, and re-layouts: 20.1 us -> 4.24 us
  Pallas kernels: 757 us -> 745 us
    pallas_call x1, Pallas kernels: 741 us -> 725 us  [both_layers(): pl.pallas_call(functools.partial(layers_kernel, count, heads, group), out...]
    unnamed x38 -> x12, local copies, waits for them, and re-layouts: 18.6 us -> 2.8 us
where the time goes in v3:
time: 763 us; the launch traced here: 752 us
  Pallas kernels  745 us (98%)
    pallas_call x1, Pallas kernels, both_layers(): pl.pallas_call(functools.partial(layers_kernel, count, heads, group), out...  725 us
    pallas_call x2, Pallas kernels, packed(): pl.pallas_call(kernel, grid=(rows // step,), out_shape=outs, in_specs=fir...  20 us

profile of v3, /device:TPU:0, one launch (start us, length us, event | category | flops | bytes accessed | tf_op | source)
XLA Modules:
  0.0 752.2 jit_solution(4373580177548978491)
XLA Ops:
  0.7 0.9 reduce_window_sum.14
  1.5 0.1 convert_reduce_fusion
  1.6 0.6 broadcast_in_dim.5.refs_11_
  2.2 0.2 fusion
  2.4 0.7 pad_maximum_fusion
  3.0 0.9 copy.20.refs_10_
  3.9 11.5 %shard_map.169 = (bf16[2,256,640]{2,1,0:T(8,128)(2,1)}, bf16[2,256,512]{2,1,0:T(8,128)(2,1)}, bf16[2,2,256,1408]{3,2,1,0:T(8,128)(2,1)}, bf16[2,2,256,768]{3,2,1,0:T(8,128)(2,1)}) custom-call(bf16[1,256,1024]{2,1,0:T(8,128)(2,1)} %w_query.1, bf16[1,256,2,128]{3,2,1,0:T(2,128)(2,1)} %keyval.1, bf16[1,256,1024]{2,1,0:T(8,128)(2,1)} %w_out.1, ...), custom_call_target="tpu_custom_call" | custom-call | tf_op jit(solution)/shard_map/pallas_call | solution.py:1139
  15.4 725.3 %shard_map.170 = (bf16[2,1,128,1024]{3,2,1,0:T(8,128)(2,1)}, bf16[2,1,128,1024]{3,2,1,0:T(8,128)(2,1)}, bf16[2,256,640]{2,1,0:T(8,128)(2,1)}, bf16[2,256,512]{2,...) custom-call(bf16[2,256,640]{2,1,0:T(8,128)(2,1)} %get-tuple-element., ...), custom_call_target="tpu_custom_call" | custom-call | tf_op jit(solution)/shard_map/pallas_call | solution.py:1048
  740.7 0.0 copy-start.1
  740.7 0.0 copy-start
  740.7 8.5 %shard_map.171 = (f32[1,256,1024]{2,1,0:T(8,128)}, f32[1,256,2,128]{3,2,1,0:T(2,128)}, f32[1,256,1024]{2,1,0:T(8,128)}, f32[1,256,2,2816]{3,2,1,0:T(2,128)}, f32[1,256,2816]{2,1,0:T(8,128)}) custom-call(bf16[2,256,640]{2,1,0:T(8,128)(2,1)} %get-tuple-element.33.qkv, bf16[2,256,512]{2,1,0:T(8,128)(2,1)} %get-tuple-element.34.out, ...), custom_call_target="tpu_custom_call" | custom-call | tf_op jit(solution)/shard_map/pallas_call | solution.py:1139
  749.2 0.0 copy-start.3
  749.2 0.0 copy-start.2
  749.2 0.0 copy-done.1
  749.3 0.8 copy.25
  750.0 0.0 copy-done
  750.0 0.8 copy.26
  750.8 0.0 copy-done.3
  750.8 0.6 copy.27
  751.4 0.0 copy-done.2
  751.4 0.6 copy.28
  (1 shorter events, 0.0 us)
Async XLA Ops:
  740.7 8.6 %copy-start.1 = (bf16[2,1,128,1024]{3,2,1,0:T(8,128)(2,1)S(1)}, bf16[2,1,128,1024]{3,2,1,0:T(8,128)(2,1)}, u32[]{:S(2)}) copy-start(bf16[2,1,128,1024]{3,2,1,0:T(8,128)(2,1)} %get-tuple-element.56) | copy-start | bytes 1572868
  740.7 9.3 %copy-start = (bf16[2,1,128,1024]{3,2,1,0:T(8,128)(2,1)S(1)}, bf16[2,1,128,1024]{3,2,1,0:T(8,128)(2,1)}, u32[]{:S(2)}) copy-start(bf16[2,1,128,1024]{3,2,1,0:T(8,128)(2,1)} %get-tuple-element.57) | copy-start | bytes 1572868
  749.2 1.6 copy-start.3
  749.2 2.2 copy-start.2

commit v4 on v3

--- a/solution.py
+++ b/solution.py
@@ -489,8 +489,8 @@
     "E01", "Z310", "Y31", "S01", "bi1", "bl0", "bk0", "S30", "E30", "bp0", "bs0", "Z113",
     "Y21", "Z302", "Z013", "bt0", "Z111", "S20", "Z110", "Z011", "E20", "Z200", "Z303", "Z012",
     "bv0", "ba0", "Z112", "be0", "Z010", "Z201", "Z301", "Y01", "Z203", "Y11", "bq0", "Z202",
-    "Z300", "E00", "S00", "E10", "br0", "bn0", "Y30", "bn1", "d1", "Z003", "bn2", "s1",
-    "S10", "Z000", "Y20", "Z002", "Z103", "Z001", "Z101", "Z102", "Z100", "t1", "Y00", "Y10",
+    "Z300", "E00", "S00", "E10", "br0", "bn0", "Y30", "bn1", "S10", "d1", "Z003", "bn2",
+    "s1", "Z000", "Y20", "Z002", "Z103", "Z001", "Z101", "Z102", "Z100", "t1", "Y00", "Y10",
     "bn3", "w1", "bn4", "v1", "bn5", "w0",
 )
 
@@ -1132,7 +1132,7 @@
 
 def packed(raw, kernel, outs, raw_first):
     rows = raw[0].shape[1] if raw_first else raw[0].shape[-2]
-    step = min(rows, 64)
+    step = min(rows, 32 if raw_first else 128)
     wide = [(block.shape, 1) for block in (raw if raw_first else outs)]
     narrow = [(block.shape, len(block.shape) - 2) for block in (outs if raw_first else raw)]
     first, second = row_specs(wide, step), row_specs(narrow, step)

time: 763 us -> 761 us (level)
  no operation moved by 1% of the time
where the time goes in v4:
time: 761 us; the launch traced here: 751 us
  Pallas kernels  744 us (98%)
    pallas_call x1, Pallas kernels, both_layers(): pl.pallas_call(functools.partial(layers_kernel, count, heads, group), out...  725 us
    pallas_call x2, Pallas kernels, packed(): pl.pallas_call(kernel, grid=(rows // step,), out_shape=outs, in_specs=fir...  18.5 us

profile of v4, /device:TPU:0, one launch (start us, length us, event | category | flops | bytes accessed | tf_op | source)
XLA Modules:
  0.0 750.7 jit_solution(9393968021666571965)
XLA Ops:
  0.7 0.9 reduce_window_sum.14
  1.5 0.1 convert_reduce_fusion
  1.6 0.6 broadcast_in_dim.5.refs_11_
  2.2 0.2 fusion
  2.4 0.7 pad_maximum_fusion
  3.0 0.9 copy.20.refs_10_
  3.9 10.6 %shard_map.169 = (bf16[2,256,640]{2,1,0:T(8,128)(2,1)}, bf16[2,256,512]{2,1,0:T(8,128)(2,1)}, bf16[2,2,256,1408]{3,2,1,0:T(8,128)(2,1)}, bf16[2,2,256,768]{3,2,1,0:T(8,128)(2,1)}) custom-call(bf16[1,256,1024]{2,1,0:T(8,128)(2,1)} %w_query.1, bf16[1,256,2,128]{3,2,1,0:T(2,128)(2,1)} %keyval.1, bf16[1,256,1024]{2,1,0:T(8,128)(2,1)} %w_out.1, ...), custom_call_target="tpu_custom_call" | custom-call | tf_op jit(solution)/shard_map/pallas_call | solution.py:1139
  14.5 725.2 %shard_map.170 = (bf16[2,1,128,1024]{3,2,1,0:T(8,128)(2,1)}, bf16[2,1,128,1024]{3,2,1,0:T(8,128)(2,1)}, bf16[2,256,640]{2,1,0:T(8,128)(2,1)}, bf16[2,256,512]{2,...) custom-call(bf16[2,256,640]{2,1,0:T(8,128)(2,1)} %get-tuple-element., ...), custom_call_target="tpu_custom_call" | custom-call | tf_op jit(solution)/shard_map/pallas_call | solution.py:1048
  739.7 0.0 copy-start.1
  739.7 0.0 copy-start
  739.7 7.9 %shard_map.171 = (f32[1,256,1024]{2,1,0:T(8,128)}, f32[1,256,2,128]{3,2,1,0:T(2,128)}, f32[1,256,1024]{2,1,0:T(8,128)}, f32[1,256,2,2816]{3,2,1,0:T(2,128)}, f32[1,256,2816]{2,1,0:T(8,128)}) custom-call(bf16[2,256,640]{2,1,0:T(8,128)(2,1)} %get-tuple-element.33.qkv, bf16[2,256,512]{2,1,0:T(8,128)(2,1)} %get-tuple-element.34.out, ...), custom_call_target="tpu_custom_call" | custom-call | tf_op jit(solution)/shard_map/pallas_call | solution.py:1139
  747.6 0.0 copy-start.3
  747.7 0.0 copy-start.2
  747.7 0.0 copy-done.1
  747.7 0.8 copy.25
  748.5 0.0 copy-done
  748.5 0.8 copy.26
  749.3 0.0 copy-done.3
  749.3 0.6 copy.27
  749.9 0.0 copy-done.2
  749.9 0.6 copy.28
  (1 shorter events, 0.0 us)
Async XLA Ops:
  739.7 8.0 %copy-start.1 = (bf16[2,1,128,1024]{3,2,1,0:T(8,128)(2,1)S(1)}, bf16[2,1,128,1024]{3,2,1,0:T(8,128)(2,1)}, u32[]{:S(2)}) copy-start(bf16[2,1,128,1024]{3,2,1,0:T(8,128)(2,1)} %get-tuple-element.56) | copy-start | bytes 1572868
  739.7 8.8 %copy-start = (bf16[2,1,128,1024]{3,2,1,0:T(8,128)(2,1)S(1)}, bf16[2,1,128,1024]{3,2,1,0:T(8,128)(2,1)}, u32[]{:S(2)}) copy-start(bf16[2,1,128,1024]{3,2,1,0:T(8,128)(2,1)} %get-tuple-element.57) | copy-start | bytes 1572868
  747.6 1.6 copy-start.3
  747.7 2.2 copy-start.2
